TPU v7x, 128 devices: a whole 4x4x4 slice. The times are simulated.
128 devices in a mesh: space: 64 (over z, y, x_hi, core), spec: 2 (over x_lo).
Axes of the slice: x: 4 (x_hi: 2, x_lo: 2; x = x_hi * 2 + x_lo), y: 4, z: 4, core: 2. Of those that a mesh axis runs over, the one named last changes fastest.
Arguments:
- spectrum: float32 [1296, 256, 512], P('spec', 'space'), may hold values from 0 to 6
- current: float32 [2, 256, 512], P(None, 'space'), may hold values from -4 to 4
- depth: float32 [256, 512], P('space'), may hold values from 8 to 4000
- wind: float32 [2, 256, 512], P(None, 'space'), may hold values from -48 to 48
- sea_blocks: int32 [256, 4], P('space'), may hold values from 0 to 1, as said below
Outputs:
- relaxed: float32 [1296, 256, 512], P('spec', 'space')
Inputs may be any that keep to these rules, and one draw needn't show every extreme that they name: `sea_blocks`: each aligned tile of 4 rows holds 1 to 8 sea blocks, and some tile holds exactly 8.
All inputs are finite; a program needn't handle non-finite values.
Results may differ from a plain program's by a relative error of at most 0.0003.
Values sent between devices are 32-bit elements; how exact they have to be, the bound alone decides.
A program may use at most 256 MiB of HBM per device.

v0:
```python
import math

import jax
import jax.numpy as jnp
from jax import lax
from jax.sharding import PartitionSpec as P

ND = 36
NF = 36


GRAVITY = 9.81
SIGMA_LOW = 2.0 * math.pi * 0.035
LOG_RATIO = math.log(1.1)
HALF_SPREAD = 0.5 * (1.1 - 1.0 / 1.1)
TIME_STEP = 140.0
CELL_WIDTH = 4600.0
SOURCE_STEP = 280.0
INPUT_COEF = 0.0002
DECAY_COEF = 0.002
STEEP_REF = 600.0
EPSILON = 1e-06


def with_halo(array, sides, width):
    for axis, dim in sides:
        size, length = (lax.axis_size(axis), array.shape[dim])
        up = [(i, (i + 1) % size) for i in range(size - 1)]
        down = [(j, i) for i, j in up]
        last = lax.slice_in_dim(array, length - width, length, axis=dim)
        leading = lax.slice_in_dim(array, 0, width, axis=dim)
        before = lax.ppermute(last, axis, up)
        after = lax.ppermute(leading, axis, down)
        array = jnp.concatenate([before, array, after], axis=dim)
    return array


def freq_sigma(freq_index):
    return SIGMA_LOW * jnp.exp(freq_index.astype(jnp.float32) * LOG_RATIO)


def dir_angle(dir_index):
    return dir_index.astype(jnp.float32) * (2.0 * math.pi / ND)


def wavenumber(sigma_freq, depth_cells):
    square = sigma_freq * sigma_freq
    wavenum = square / GRAVITY / jnp.sqrt(jnp.tanh(square * depth_cells / GRAVITY))
    product = wavenum * depth_cells
    damping = jnp.exp(-2.0 * product)
    shallow = 4.0 * product * damping / (1.0 - damping * damping)
    group_speed = 0.5 * (sigma_freq / wavenum) * (1.0 + shallow)
    return (wavenum, group_speed)


def minmod(slope_one, slope_two):
    smaller = jnp.sign(slope_one) * jnp.minimum(jnp.abs(slope_one), jnp.abs(slope_two))
    return jnp.where(slope_one * slope_two > 0.0, smaller, 0.0)


def window(values, offset, length, along_axis):
    return lax.slice_in_dim(values, offset, offset + length, axis=along_axis)


def advect_axis(field_ext, speed_ext, along_axis):
    interior = field_ext.shape[along_axis] - 4
    step_ratio = TIME_STEP / CELL_WIDTH
    differences = window(field_ext, 1, interior + 3, along_axis) - window(
        field_ext, 0, interior + 3, along_axis
    )
    face_speed = 0.5 * (
        window(speed_ext, 1, interior + 1, along_axis)
        + window(speed_ext, 2, interior + 1, along_axis)
    )
    courant = face_speed * step_ratio
    slope_up = minmod(
        window(differences, 1, interior + 1, along_axis),
        window(differences, 0, interior + 1, along_axis),
    )
    slope_down = minmod(
        window(differences, 2, interior + 1, along_axis),
        window(differences, 1, interior + 1, along_axis),
    )
    face_up = window(field_ext, 1, interior + 1, along_axis) + 0.5 * (1.0 - courant) * slope_up
    face_down = window(field_ext, 2, interior + 1, along_axis) - 0.5 * (1.0 + courant) * slope_down
    fluxes = face_speed * jnp.where(face_speed >= 0.0, face_up, face_down)
    return window(field_ext, 2, interior, along_axis) - step_ratio * (
        window(fluxes, 1, interior, along_axis) - window(fluxes, 0, interior, along_axis)
    )


def pad_axis(values, along_axis):
    widths = [(0, 0)] * values.ndim
    widths[along_axis] = (2, 2)
    return jnp.pad(values, widths)


def substep(field_ext, speed_x_ext, speed_y, sea_cells):
    moved_rows = advect_axis(field_ext, speed_x_ext, 1) * sea_cells
    return advect_axis(pad_axis(moved_rows, 2), pad_axis(speed_y, 2), 2) * sea_cells


def apply_rates(
    spectra, sigma_freq, cosine, sine, wavenum, energy_sum, over_sigma, over_root, wind_x, wind_y
):
    mean_sigma = (energy_sum + EPSILON) / (over_sigma + EPSILON)
    mean_wavenum = ((energy_sum + EPSILON) / (over_root + EPSILON)) ** 2
    steepness = energy_sum * mean_wavenum**2
    decay_rate = DECAY_COEF * mean_sigma * (wavenum / mean_wavenum) * (steepness / STEEP_REF) ** 2
    wind_along = wind_x * cosine + wind_y * sine
    growth = INPUT_COEF * sigma_freq * jnp.maximum(wind_along * wavenum / sigma_freq - 1.0, 0.0)
    return spectra * (1.0 + SOURCE_STEP * growth) / (1.0 + SOURCE_STEP * decay_rate)


def source_terms(spectra, depth_cells, wind_x, wind_y):
    ones_tail = (1,) * depth_cells.ndim
    sigma_freq = freq_sigma(jnp.arange(NF, dtype=jnp.int32)).reshape((NF,) + ones_tail)
    direction_angle = dir_angle(jnp.arange(ND, dtype=jnp.int32)).reshape((ND, 1) + ones_tail)
    wavenum, group_unused = wavenumber(sigma_freq, depth_cells[None])
    energy = spectra * (sigma_freq * sigma_freq * HALF_SPREAD * (2.0 * math.pi / ND))
    energy_sum = jnp.sum(energy, axis=(0, 1))
    over_sigma = jnp.sum(energy / sigma_freq, axis=(0, 1))
    over_root = jnp.sum(energy / jnp.sqrt(wavenum), axis=(0, 1))
    return apply_rates(
        spectra,
        sigma_freq,
        jnp.cos(direction_angle),
        jnp.sin(direction_angle),
        wavenum,
        energy_sum,
        over_sigma,
        over_root,
        wind_x,
        wind_y,
    )


def on_device(spectrum, current, depth, wind, sea_blocks):
    bins_local, rows_local, cols_local = spectrum.shape
    spec_index = lax.axis_index("spec")
    spec_count = lax.axis_size("spec")
    global_bin = spec_index * bins_local + jnp.arange(bins_local, dtype=jnp.int32)
    sigma_bin = freq_sigma(global_bin % NF).reshape(bins_local, 1, 1)
    angle_bin = dir_angle(global_bin // NF).reshape(bins_local, 1, 1)
    cosine = jnp.cos(angle_bin)
    sine = jnp.sin(angle_bin)
    sea_cells = jnp.repeat(sea_blocks, 128, axis=1).astype(jnp.float32)
    fields = jnp.stack([current[0], current[1], depth, sea_cells])

    def speeds(fields_ext):
        depth_ext = fields_ext[2][None]
        inside = depth_ext > 0.0
        wavenum_unused, group_speed = wavenumber(sigma_bin, jnp.where(inside, depth_ext, 1.0))
        speed_x = jnp.where(inside, group_speed * cosine + fields_ext[0][None], 0.0)
        speed_y = jnp.where(inside, group_speed * sine + fields_ext[1][None], 0.0)
        return (speed_x, speed_y)

    def advance(spectra_now):
        extended = with_halo(jnp.concatenate([spectra_now, fields], axis=0), (("space", 1),), 2)
        speed_x, speed_y = speeds(extended[bins_local:])
        return substep(extended[:bins_local], speed_x, speed_y[:, 2:-2], sea_cells[None])

    propagated = advance(advance(spectrum))
    blocks_tile = rows_local * cols_local // 128
    flat = propagated.reshape(bins_local, blocks_tile, 128)
    depth_blocks = depth.reshape(blocks_tile, 128)
    wind_blocks = wind.reshape(2, blocks_tile, 128)
    per_device = blocks_tile // spec_count
    points = lax.all_to_all(flat, "spec", split_axis=1, concat_axis=0, tiled=True)
    block_ids = spec_index * per_device + jnp.arange(per_device, dtype=jnp.int32)
    depth_pick = jnp.take(depth_blocks, block_ids, axis=0)
    wind_pick = jnp.take(wind_blocks, block_ids, axis=1)
    point_blocks = points.shape[1]
    spectra = points.reshape(ND, NF, point_blocks, 128)
    relaxed_here = source_terms(spectra, depth_pick, wind_pick[0], wind_pick[1])
    result = lax.all_to_all(
        relaxed_here.reshape(ND * NF, point_blocks, 128),
        "spec",
        split_axis=0,
        concat_axis=1,
        tiled=True,
    )
    return result.reshape(bins_local, rows_local, cols_local)


def solution(mesh):
    placed = (
        P("spec", "space", None),
        P(None, "space", None),
        P("space", None),
        P(None, "space", None),
        P("space", None),
    )
    return jax.shard_map(
        on_device, mesh=mesh, in_specs=placed, out_specs=P("spec", "space", None), check_vma=False
    )
```

profile of v0, /device:TPU:4, one launch (start us, length us, event | category | flops | bytes accessed | tf_op | source)
XLA Modules:
  0.0 615.8 jit_solution(2599132272020785880)
XLA Ops:
  0.0 0.7 convert_element_type.91
  0.7 0.1 broadcast_in_dim.79
  0.8 10.3 %pad_maximum_fusion.19 = f32[652,4,512]{2,1,0:T(4,128)S(1)} fusion(f32[1,4,512]{2,1,0:T(4,128)S(1)} %convert_element_type.92, f32[1,4,512]{2,1,0:T(4,128)} %bitcast.77, f32[2,4,512]{2,1,0:T(4,128)} %param.6, f32[648,4,512]{2,1,0:T(4,128)} %param.5), kind=kLoop, calls=%fused_computation.49 | loop fusion | flops 4005888 | bytes 10682368 | tf_op jit(solution)/shard_map/concatenate | solution.py:159
  11.1 2.1 fusion.64
  13.1 2.0 copy.19
  15.2 1.9 collective-permute-start
  17.1 2.0 copy.20
  19.1 5.3 collective-permute-start.1
  24.4 0.1 broadcast_bitcast_fusion
  24.6 26.1 %collective-permute-done = f32[652,2,512]{2,0,1:T(8,128)} collective-permute-done((f32[652,2,512]{2,0,1:T(8,128)}, f32[652,2,512]{2,0,1:T(8,128)}, u32[]{:S(2)}, u32[]{:S(2)}) %collective-permute-start) | collective-permute-done | bytes 2670624 | tf_op jit(solution)/shard_map/ppermute | solution.py:32
  50.7 3.8 copy.21
  54.5 22.5 %collective-permute-done.1 = f32[652,2,512]{2,0,1:T(8,128)} collective-permute-done((f32[652,2,512]{2,0,1:T(8,128)}, f32[652,2,512]{2,0,1:T(8,128)}, u32[]{:S(2)}, u32[]{:S(2)}) %collective-permute-start.1) | collective-permute-done | bytes 2670624 | tf_op jit(solution)/shard_map/ppermute | solution.py:33
  77.0 3.8 copy.22
  80.9 13.4 %fusion.1 = f32[652,8,512]{2,1,0:T(8,128)S(1)} fusion(f32[1,4,512]{2,1,0:T(4,128)S(1)} %convert_element_type.92, f32[1,4,512]{2,1,0:T(4,128)S(1)} %bitcast.78, f32[2,4,512]{2,1,0:T(4,128)S(1)} %copy-done.6, f32[652,2,512]{2,1,0:T(2,128)S(1)} %copy.22, f32[648,4,512]{2,1,0:T(4,128)S(1)} %bitcast.74, f32[652,2,512]{2,1,0:T(2,128)S(1)} %copy.21), kind=kLoop, calls=%fused_computation.21 | loop fusion | flops 13352960 | bytes 21364736 | tf_op jit(solution)/shard_map/concatenate | solution.py:34
  94.3 1.4 slice_subtract_fusion.1
  95.7 14.1 %add_multiply_fusion.1 = (f32[648,8,512]{2,1,0:T(8,128)}, f32[648,8,512]{2,1,0:T(8,128)}) fusion(f32[8,512]{1,0:T(8,128)S(1)} %get-tuple-element.12, f32[648]{0:T(1024)S(1)} %get-tuple-element.32, f32[648]{0:T(1024)S(1)} %get-tuple-element.30, f32[648]{0:T(1024)S(1)} %get-tuple-element.29, f32[8,512]{1,0:T(8,128)S(1)} %get-tuple-element.13, ...), kind=kLoop, calls=%fused_computation.47 | loop fusion | flops 45121536 | bytes 21280896 | tf_op jit(solution)/shard_map/mul | solution.py:52
  109.9 36.3 %fusion.7 = f32[648,5,512]{2,1,0:T(8,128)} fusion(f32[1,4,512]{2,1,0:T(4,128)S(1)} %convert_element_type.92, f32[1,4,512]{2,1,0:T(4,128)S(1)} %bitcast.79, f32[2,4,512]{2,1,0:T(4,128)S(1)} %copy-done.6, f32[652,2,512]{2,1,0:T(2,128)} %copy-done.5, f32[648,4,512]{2,1,0:T(4,128)S(1)} %bitcast.74, f32[652,2,512]{2,1,0:T(2,128)} %copy-done.3, ...), kind=kLoop, calls=%fused_computation.27 | loop fusion | flops 61378560 | bytes 50495488 | tf_op jit(solution)/shard_map/mul | solution.py:86
  146.2 13.0 %fusion.31 = f32[648,4,512]{2,1,0:T(4,128)} fusion(f32[648,4,512]{2,1,0:T(4,128)S(1)} %bitcast.74, f32[648,5,512]{2,1,0:T(8,128)} %fusion.7, f32[4,512]{1,0:T(4,128)S(1)} %bitcast.83), kind=kLoop, calls=%fused_computation.85 | loop fusion | flops 5308416 | bytes 21241856 | tf_op jit(solution)/shard_map/mul | solution.py:99
  159.2 13.7 %slice_subtract_fusion.3 = f32[648,4,515]{2,1,0:T(4,128)} fusion(f32[648,4,512]{2,1,0:T(4,128)} %fusion.31), kind=kLoop, calls=%fused_computation.62 | loop fusion | flops 1334880 | bytes 10647936 | tf_op jit(solution)/shard_map/sub | solution.py:68
  173.0 6.6 %fusion.28 = f32[648,4,512]{2,1,0:T(4,128)S(1)} fusion(f32[648,8,512]{2,1,0:T(8,128)} %get-tuple-element.20, f32[4,512]{1,0:T(4,128)S(1)} %slice.289, f32[648]{0:T(1024)S(1)} %fusion.54, pred[4,512]{1,0:T(4,128)(4,1)S(1)} %slice.290), kind=kLoop, calls=%fused_computation.81 | loop fusion | flops 3981312 | bytes 10629664 | tf_op jit(solution)/shard_map/jit(_where)/select_n | solution.py:155
  179.6 21.8 %select_multiply_fusion.1 = f32[648,4,513]{2,1,0:T(4,128)S(1)} fusion(f32[648,4,515]{2,1,0:T(4,128)S(1)} %copy-done.1, f32[648,4,512]{2,1,0:T(4,128)S(1)} %fusion.28, f32[648,4,512]{2,1,0:T(4,128)} %fusion.31), kind=kLoop, calls=%fused_computation.59 | loop fusion | flops 38561184 | bytes 31891968 | tf_op jit(solution)/shard_map/mul | solution.py:86
  201.4 3.0 fusion.26
  204.5 9.3 %pad_maximum_fusion.18 = f32[652,4,512]{2,1,0:T(4,128)S(1)} fusion(f32[1,4,512]{2,1,0:T(4,128)S(1)} %convert_element_type.92, f32[1,4,512]{2,1,0:T(4,128)S(1)} %bitcast.80, f32[2,4,512]{2,1,0:T(4,128)S(1)} %copy-done.6, f32[648,4,512]{2,1,0:T(4,128)S(1)} %fusion.26), kind=kLoop, calls=%fused_computation.48 | loop fusion | flops 4005888 | bytes 10682368 | tf_op jit(solution)/shard_map/concatenate | solution.py:159
  213.7 3.6 fusion.63
  217.3 2.3 copy.25
  219.6 5.2 collective-permute-start.2
  224.8 0.5 copy.26
  225.3 2.0 collective-permute-start.3
  227.4 27.6 %collective-permute-done.2 = f32[652,2,512]{2,0,1:T(8,128)S(1)} collective-permute-done((f32[652,2,512]{2,0,1:T(8,128)S(1)}, f32[652,2,512]{2,0,1:T(8,128)S(1)}, u32[]{:S(2)}, u32[]{:S(2)}) %collective-permute-start.2) | collective-permute-done | bytes 2670624 | tf_op jit(solution)/shard_map/ppermute | solution.py:32
  254.9 2.1 copy.27
  257.0 25.8 %collective-permute-done.3 = f32[652,2,512]{2,0,1:T(8,128)S(1)} collective-permute-done((f32[652,2,512]{2,0,1:T(8,128)S(1)}, f32[652,2,512]{2,0,1:T(8,128)S(1)}, u32[]{:S(2)}, u32[]{:S(2)}) %collective-permute-start.3) | collective-permute-done | bytes 2670624 | tf_op jit(solution)/shard_map/ppermute | solution.py:33
  282.8 2.1 copy.28
  284.8 13.3 %fusion.3 = f32[652,8,512]{2,1,0:T(8,128)S(1)} fusion(f32[1,4,512]{2,1,0:T(4,128)S(1)} %convert_element_type.92, f32[1,4,512]{2,1,0:T(4,128)S(1)} %bitcast.81, f32[2,4,512]{2,1,0:T(4,128)S(1)} %copy-done.6, f32[652,2,512]{2,1,0:T(2,128)S(1)} %copy.28, f32[648,4,512]{2,1,0:T(4,128)S(1)} %fusion.26, f32[652,2,512]{2,1,0:T(2,128)S(1)} %copy.27), kind=kLoop, calls=%fused_computation.23 | loop fusion | flops 13352960 | bytes 21364736 | tf_op jit(solution)/shard_map/concatenate | solution.py:34
  298.2 1.4 slice_subtract_fusion
  299.7 14.1 %add_multiply_fusion = (f32[648,8,512]{2,1,0:T(8,128)}, f32[648,8,512]{2,1,0:T(8,128)}) fusion(f32[8,512]{1,0:T(8,128)S(1)} %get-tuple-element.9, f32[648]{0:T(1024)S(1)} %get-tuple-element.32, f32[648]{0:T(1024)S(1)} %get-tuple-element.30, f32[648]{0:T(1024)S(1)} %get-tuple-element.29, f32[8,512]{1,0:T(8,128)S(1)} %get-tuple-element.10, ...), kind=kLoop, calls=%fused_computation.43 | loop fusion | flops 45121536 | bytes 21280896 | tf_op jit(solution)/shard_map/mul | solution.py:52
  313.8 36.3 %fusion.11 = f32[648,5,512]{2,1,0:T(8,128)} fusion(f32[1,4,512]{2,1,0:T(4,128)S(1)} %convert_element_type.92, f32[1,4,512]{2,1,0:T(4,128)S(1)} %bitcast.82, f32[2,4,512]{2,1,0:T(4,128)S(1)} %copy-done.6, f32[652,2,512]{2,1,0:T(2,128)} %copy-done.4, f32[648,4,512]{2,1,0:T(4,128)S(1)} %fusion.26, f32[652,2,512]{2,1,0:T(2,128)} %copy-done.2, ...), kind=kLoop, calls=%fused_computation.31 | loop fusion | flops 61378560 | bytes 50495488 | tf_op jit(solution)/shard_map/mul | solution.py:86
  350.1 13.0 %fusion.23 = f32[648,4,512]{2,1,0:T(4,128)} fusion(f32[648,4,512]{2,1,0:T(4,128)S(1)} %fusion.26, f32[648,5,512]{2,1,0:T(8,128)} %fusion.11, f32[4,512]{1,0:T(4,128)S(1)} %bitcast.85), kind=kLoop, calls=%fused_computation.74 | loop fusion | flops 5308416 | bytes 21241856 | tf_op jit(solution)/shard_map/mul | solution.py:99
  363.2 13.7 %slice_subtract_fusion.2 = f32[648,4,515]{2,1,0:T(4,128)} fusion(f32[648,4,512]{2,1,0:T(4,128)} %fusion.23), kind=kLoop, calls=%fused_computation.57 | loop fusion | flops 1334880 | bytes 10647936 | tf_op jit(solution)/shard_map/sub | solution.py:68
  376.9 6.6 %fusion.20 = f32[648,4,512]{2,1,0:T(4,128)S(1)} fusion(f32[648,8,512]{2,1,0:T(8,128)} %get-tuple-element.18, f32[4,512]{1,0:T(4,128)S(1)} %slice.311, f32[648]{0:T(1024)S(1)} %fusion.54, pred[4,512]{1,0:T(4,128)(4,1)S(1)} %slice.312), kind=kLoop, calls=%fused_computation.70 | loop fusion | flops 3981312 | bytes 10629664 | tf_op jit(solution)/shard_map/jit(_where)/select_n | solution.py:155
  383.5 21.8 %select_multiply_fusion = f32[648,4,513]{2,1,0:T(4,128)S(1)} fusion(f32[648,4,515]{2,1,0:T(4,128)S(1)} %copy-done, f32[648,4,512]{2,1,0:T(4,128)S(1)} %fusion.20, f32[648,4,512]{2,1,0:T(4,128)} %fusion.23), kind=kLoop, calls=%fused_computation.54 | loop fusion | flops 38561184 | bytes 31891968 | tf_op jit(solution)/shard_map/mul | solution.py:86
  405.4 4.4 fusion.18
  409.8 7.7 %reshape.215 = f32[648,16,128]{2,1,0:T(8,128)} reshape(f32[648,4,512]{2,1,0:T(4,128)} %fusion.18) | data formatting | bytes 10616832 | tf_op jit(solution)/shard_map/reshape | solution.py:165
  417.5 6.6 %copy.31 = f32[648,16,128]{2,0,1:T(8,128)} copy(f32[648,16,128]{2,1,0:T(8,128)} %reshape.215) | data formatting | bytes 10616832 | tf_op jit(solution)/shard_map/reshape | solution.py:165
  424.1 6.1 all-to-all-start
  430.3 0.1 div.183
  430.4 0.1 mul.764
  430.5 0.6 gather_fusion.1
  431.1 0.6 gather_fusion
  431.7 0.1 div.179
  431.8 0.1 mul.734
  432.0 0.1 broadcast_select_fusion
  432.0 0.1 select_bitcast_fusion
  432.1 0.2 fusion.40
  432.3 0.1 multiply_add_fusion.1
  432.4 58.6 %all-to-all-done = f32[648,16,128]{2,0,1:T(8,128)} async-done(((f32[648,16,128]{2,0,1:T(8,128)}), f32[648,16,128]{2,0,1:T(8,128)}, u32[]{:S(2)}, u32[]{:S(2)}) %all-to-all-start) | async-done | bytes 5308448 | tf_op jit(solution)/shard_map/all_to_all | solution.py:169
  491.0 3.5 copy.33
  494.6 0.6 div.187
  495.2 9.1 %divide_reduce_fusion = (f32[8,128]{1,0:T(8,128)S(1)}, f32[8,128]{1,0:T(8,128)S(1)}, f32[8,128]{1,0:T(8,128)S(1)}) fusion(f32[648,16,128]{2,0,1:T(8,128)} %all-to-all-done, f32[648]{0:T(1024)S(1)} %div.183, f32[648]{0:T(1024)S(1)} %mul.764, f32[2,648,8,128]{3,2,1,0:T(8,128)S(1)} %bitcast.75), kind=kLoop, calls=%fused_computation.96 | loop fusion | flops 7959552 | bytes 10634304 | tf_op jit(solution)/shard_map/reduce_sum | solution.py:122
  504.3 0.1 multiply_add_fusion
  504.4 0.6 broadcast_multiply_fusion
  505.0 37.2 %bitcast_divide_fusion = f32[1296,8,128]{2,1,0:T(8,128)S(1)} fusion(f32[36,36,8,128]{3,2,1,0:T(8,128)S(1)} %broadcast_multiply_fusion, f32[2,648,8,128]{3,2,1,0:T(8,128)S(1)} %copy.33, f32[36,8,128]{2,1,0:T(8,128)S(1)} %get-tuple-element.26, f32[1296]{0:T(1024)S(1)} %div.179, f32[1296]{0:T(1024)S(1)} %mul.734), kind=kLoop, calls=%fused_computation.86 | loop fusion | flops 10616832 | bytes 16083072 | tf_op jit(solution)/shard_map/div | solution.py:112
  542.2 63.3 %all_to_all.30 = f32[1296,8,128]{2,1,0:T(8,128)S(1)} all-to-all(f32[1296,8,128]{2,1,0:T(8,128)S(1)} %bitcast_divide_fusion), channel_id=1, replica_groups=mesh['space'=64,'spec'=2] {'spec'}, dimensions={0} | all-to-all | bytes 10616832 | tf_op jit(solution)/shard_map/all_to_all | solution.py:176
  605.6 2.8 copy.36
  608.3 7.2 %reshape.219 = f32[648,4,512]{2,1,0:T(4,128)} reshape(f32[648,2,8,128]{3,2,1,0:T(8,128)} %copy.36) | data formatting | bytes 10616832 | tf_op jit(solution)/shard_map/reshape | solution.py:183
  (63 shorter events, 0.5 us)
Async XLA Ops:
  15.2 35.5 %collective-permute-start = (f32[652,2,512]{2,0,1:T(8,128)}, f32[652,2,512]{2,0,1:T(8,128)}, u32[]{:S(2)}, u32[]{:S(2)}) collective-permute-start(f32[652,2,512]{2,0,1:T(8,128)} %copy.19), channel_id=1, source_target_pairs={{0,2},{2,4},{4,6},{6,8},{8,10},{10,12},{12,14},{14,16},{16,18},{18... | collective-permute-start | bytes 8011784 | tf_op jit(solution)/shard_map/ppermute | solution.py:32
  19.1 61.7 %slice-start.4 = ((s8[5308416]{0:T(1024)(128)(4,1)}), s8[1114112]{0:T(1024)(128)(4,1)S(1)}, s32[]{:S(2)}) async-start(s8[5308416]{0:T(1024)(128)(4,1)} %bitcast.73), calls=%async_computation.6 | async-start | bytes 2228224
  19.1 61.7 %copy-start.6 = (f32[2,4,512]{2,1,0:T(4,128)S(1)}, f32[2,4,512]{2,1,0:T(4,128)}, u32[]{:S(2)}) copy-start(f32[2,4,512]{2,1,0:T(4,128)} %param.6) | copy-start | bytes 49156
  19.1 61.7 %copy-start.7 = (f32[4,512]{1,0:T(4,128)S(1)}, f32[4,512]{1,0:T(4,128)}, u32[]{:S(2)}) copy-start(f32[4,512]{1,0:T(4,128)} %param.7) | copy-start | bytes 24580
  19.1 57.9 %collective-permute-start.1 = (f32[652,2,512]{2,0,1:T(8,128)}, f32[652,2,512]{2,0,1:T(8,128)}, u32[]{:S(2)}, u32[]{:S(2)}) collective-permute-start(f32[652,2,512]{2,0,1:T(8,128)} %copy.20), channel_id=1, source_target_pairs={{2,0},{4,2},{6,4},{8,6},{10,8},{12,10},{14,12},{16,14},{18,16},{20... | collective-permute-start | bytes 8011784 | tf_op jit(solution)/shard_map/ppermute | solution.py:33
  24.6 56.2 %slice-start.5 = ((s8[5308416]{0:T(1024)(128)(4,1)}), s8[4194304]{0:T(1024)(128)(4,1)S(1)}, s32[]{:S(2)}) async-start(s8[5308416]{0:T(1024)(128)(4,1)} %bitcast.73), calls=%async_computation.7 | async-start | bytes 8388608
  54.5 39.8 %copy-start.3 = (f32[652,2,512]{2,1,0:T(2,128)}, f32[652,2,512]{2,1,0:T(2,128)S(1)}, u32[]{:S(2)}) copy-start(f32[652,2,512]{2,1,0:T(2,128)S(1)} %copy.21) | copy-start | bytes 8011780
  80.9 13.4 %copy-start.5 = (f32[652,2,512]{2,1,0:T(2,128)}, f32[652,2,512]{2,1,0:T(2,128)S(1)}, u32[]{:S(2)}) copy-start(f32[652,2,512]{2,1,0:T(2,128)S(1)} %copy.22) | copy-start | bytes 8011780
  173.0 6.6 %copy-start.1 = (f32[648,4,515]{2,1,0:T(4,128)S(1)}, f32[648,4,515]{2,1,0:T(4,128)}, u32[]{:S(2)}) copy-start(f32[648,4,515]{2,1,0:T(4,128)} %slice_subtract_fusion.3) | copy-start | bytes 16018564
  173.0 28.4 %slice-start.2 = ((s8[5308416]{0:T(1024)(128)(4,1)}), s8[4194304]{0:T(1024)(128)(4,1)S(1)}, s32[]{:S(2)}) async-start(s8[5308416]{0:T(1024)(128)(4,1)} %bitcast.71), calls=%async_computation.4 | async-start | bytes 8388608
  179.6 21.8 %slice-start.3 = ((s8[5308416]{0:T(1024)(128)(4,1)}), s8[1114112]{0:T(1024)(128)(4,1)S(1)}, s32[]{:S(2)}) async-start(s8[5308416]{0:T(1024)(128)(4,1)} %bitcast.71), calls=%async_computation.5 | async-start | bytes 2228224
  219.6 35.4 %collective-permute-start.2 = (f32[652,2,512]{2,0,1:T(8,128)S(1)}, f32[652,2,512]{2,0,1:T(8,128)S(1)}, u32[]{:S(2)}, u32[]{:S(2)}) collective-permute-start(f32[652,2,512]{2,0,1:T(8,128)S(1)} %copy.25), channel_id=1, source_target_pairs={{0,2},{2,4},{4,6},{6,8},{8,10},{10,12},{12,14},{14,16},{16,18},{18... | collective-permute-start | bytes 8011784 | tf_op jit(solution)/shard_map/ppermute | solution.py:32
  225.3 57.5 %collective-permute-start.3 = (f32[652,2,512]{2,0,1:T(8,128)S(1)}, f32[652,2,512]{2,0,1:T(8,128)S(1)}, u32[]{:S(2)}, u32[]{:S(2)}) collective-permute-start(f32[652,2,512]{2,0,1:T(8,128)S(1)} %copy.26), channel_id=1, source_target_pairs={{2,0},{4,2},{6,4},{8,6},{10,8},{12,10},{14,12},{16,14},{18,16},{20... | collective-permute-start | bytes 8011784 | tf_op jit(solution)/shard_map/ppermute | solution.py:33
  257.0 41.2 %copy-start.2 = (f32[652,2,512]{2,1,0:T(2,128)}, f32[652,2,512]{2,1,0:T(2,128)S(1)}, u32[]{:S(2)}) copy-start(f32[652,2,512]{2,1,0:T(2,128)S(1)} %copy.27) | copy-start | bytes 8011780
  284.8 13.3 %copy-start.4 = (f32[652,2,512]{2,1,0:T(2,128)}, f32[652,2,512]{2,1,0:T(2,128)S(1)}, u32[]{:S(2)}) copy-start(f32[652,2,512]{2,1,0:T(2,128)S(1)} %copy.28) | copy-start | bytes 8011780
  376.9 6.6 %copy-start = (f32[648,4,515]{2,1,0:T(4,128)S(1)}, f32[648,4,515]{2,1,0:T(4,128)}, u32[]{:S(2)}) copy-start(f32[648,4,515]{2,1,0:T(4,128)} %slice_subtract_fusion.2) | copy-start | bytes 16018564
  376.9 28.4 %slice-start = ((s8[5308416]{0:T(1024)(128)(4,1)}), s8[4194304]{0:T(1024)(128)(4,1)S(1)}, s32[]{:S(2)}) async-start(s8[5308416]{0:T(1024)(128)(4,1)} %bitcast.69), calls=%async_computation.2 | async-start | bytes 8388608
  383.5 21.8 %slice-start.1 = ((s8[5308416]{0:T(1024)(128)(4,1)}), s8[1114112]{0:T(1024)(128)(4,1)S(1)}, s32[]{:S(2)}) async-start(s8[5308416]{0:T(1024)(128)(4,1)} %bitcast.69), calls=%async_computation.3 | async-start | bytes 2228224
  424.1 6.3 %copy-start.8 = (f32[2,4,512]{2,1,0:T(4,128)S(1)}, f32[2,4,512]{2,1,0:T(4,128)}, u32[]{:S(2)}) copy-start(f32[2,4,512]{2,1,0:T(4,128)} %param.8) | copy-start | bytes 49156
  424.1 66.9 %all-to-all-start = ((f32[648,16,128]{2,0,1:T(8,128)}), f32[648,16,128]{2,0,1:T(8,128)}, u32[]{:S(2)}, u32[]{:S(2)}) async-start(f32[648,16,128]{2,0,1:T(8,128)} %copy.31), calls=%async_computation | async-start | bytes 10616832 | tf_op jit(solution)/shard_map/all_to_all | solution.py:169
where the time goes:
time: 626 us; the launch traced here: 616 us
  other arithmetic  316 us (50%)
  waiting for transfers between devices  160 us (26%)
  blocking collectives  63.3 us (10%)
  local copies, waits for them, and re-layouts  54.5 us (9%)
  starting transfers between devices  20.5 us (3%)
    mul x4, other arithmetic, advect_axis(): fluxes = face_speed * jnp.where(face_speed >= 0.0, face_up, face_down)  116 us
    all_to_all x1, blocking collectives, on_device(): lax.all_to_all(relaxed_here.reshape(ND * NF, point_blocks, 128), 'spec',...  63.3 us
    all_to_all x1, waiting for transfers between devices, on_device(): lax.all_to_all(flat, 'spec', split_axis=1, concat_axis=0, tiled=True)  58.6 us
    ppermute x2, waiting for transfers between devices, with_halo(): before = lax.ppermute(last, axis, up)  53.6 us
    ppermute x2, waiting for transfers between devices, with_halo(): after = lax.ppermute(leading, axis, down)  48.3 us
    div x1, other arithmetic, apply_rates(): spectra * (1.0 + SOURCE_STEP * growth) / (1.0 + SOURCE_STEP * decay_rate)  37.2 us
    sub x4, other arithmetic, advect_axis(): window(field_ext, 1, interior + 3, along_axis)  30.3 us
    mul x2, other arithmetic, wavenumber(): group_speed = 0.5 * (sigma_freq / wavenum) * (1.0 + shallow)  28.3 us
  transfers between devices with their start and end apart: 5, of which 5 were waited for; matrix products, arithmetic and copies ran while one was open for 2% of the time, Pallas kernels for 0%

commit v1 on v0

v1 whole, which is shorter than its diff:
```python
import functools
import math

import jax
import jax.numpy as jnp
import numpy as np
from jax import lax
from jax.experimental import pallas as pl
from jax.experimental.pallas import tpu as pltpu
from jax.sharding import PartitionSpec as P

MESH = pl.DeviceIdType.MESH
ND = 36
NF = 36
GRAVITY = 9.81
SIGMA_LOW = 2.0 * math.pi * 0.035
LOG_RATIO = math.log(1.1)
HALF_SPREAD = 0.5 * (1.1 - 1.0 / 1.1)
STEP_RATIO = 140.0 / 4600.0
SOURCE_STEP = 280.0
INPUT_COEF = 0.0002
DECAY_COEF = 0.002
STEEP_REF = 600.0
EPSILON = 1e-06

LINE = 4
LANES = 128
SLOTS = 8
GROUPS = 81
SLICE = 21
STRIDE = 20
CHUNK = 3
CHUNKS = SLICE // CHUNK
PHASES = 9
TILES = LINE + 2
BLOCKS = 16
CHUNK_ROWS = CHUNK * 8 * BLOCKS
PACK_ROWS = CHUNK * SLOTS * 8
AHEAD = 2


def phase_table(values):
    index = (np.arange(PHASES)[:, None] * 8 + np.arange(8)[None, :]) % NF
    table = values[index].astype(np.float32)
    return np.broadcast_to(table[:, :, None], (PHASES, 8, LANES)).copy()


def sigma_values():
    return SIGMA_LOW * np.exp(np.arange(NF, dtype=np.float64) * LOG_RATIO)


def wide(block):
    return jnp.concatenate([block] * 4, axis=1)


def minmod(a, b):
    return jnp.maximum(jnp.minimum(a, b), 0.0) + jnp.minimum(jnp.maximum(a, b), 0.0)


def face_flux(v, near, far, slope, slope_before, slope_after):
    up = v >= 0.0
    base = jnp.where(up, near, far)
    limited = minmod(slope, jnp.where(up, slope_before, slope_after))
    half = jnp.where(up, 0.5, -0.5) - 0.5 * v
    return v * (base + half * limited)


def wave_number(square, depth):
    return square * (1.0 / GRAVITY) / jnp.sqrt(jnp.tanh(square * depth * (1.0 / GRAVITY)))


def move_kernel(
    lines,
    spectrum,
    fields,
    ids,
    ids_here,
    trig,
    sigma,
    packed_out,
    sums_out,
    arrived,
    field_in,
    ids_in,
    ids_near,
    cg,
    cg_rows,
    cg_cols,
    cur_cols_left,
    cur_rows,
    cur_cols,
    sea,
    moved,
    done,
    packed,
    root,
    sums_mine,
    sums_other,
    in_send,
    in_recv,
    halo_send,
    halo_recv,
    back_send,
    back_recv,
    field_send,
    field_recv,
    fhalo_send,
    fhalo_recv,
    ids_send,
    ids_recv,
    sum_send,
    sum_recv,
    local_sem,
):
    space = lax.axis_index("space")
    half = lax.axis_index("spec")
    other = 1 - half
    line = space // LINE
    place = lax.rem(space, LINE)
    above = (lax.rem(line + lines - 1, lines) * LINE + place, half)
    below = (lax.rem(line + 1, lines) * LINE + place, half)
    members = [(line * LINE + s, other) for s in range(LINE)]

    barrier = pltpu.get_barrier_semaphore()
    for peer in members + [above, below]:
        pl.semaphore_signal(barrier, inc=1, device_id=peer, device_id_type=MESH)
    pl.semaphore_wait(barrier, LINE + 2)

    def remote(src, dst, send, recv, device):
        return pltpu.make_async_remote_copy(
            src_ref=src, dst_ref=dst, send_sem=send, recv_sem=recv, device_id=device, device_id_type=MESH
        )

    def into(k, s, sender):
        start = pl.multiple_of((STRIDE * s * 8 + k * CHUNK * 8) * BLOCKS, 8)
        return remote(
            spectrum.at[pl.ds(start, CHUNK_ROWS)],
            arrived.at[k, 1 + sender],
            in_send.at[k, s],
            in_recv.at[k, sender],
            members[s],
        )

    def halo(k, down):
        tile, target, device = (LINE, 0, below) if down else (1, LINE + 1, above)
        side = 0 if down else 1
        return remote(
            arrived.at[k, tile], arrived.at[k, target], halo_send.at[k, side], halo_recv.at[k, side], device
        )

    def back(k, i, sender):
        return remote(
            packed.at[i, k], packed_out.at[sender, k], back_send.at[k, i], back_recv.at[k, sender], members[i]
        )

    def field_into(s, sender):
        return remote(fields, field_in.at[1 + sender], field_send.at[s], field_recv.at[sender], members[s])

    def ids_into(s, sender):
        return remote(ids, ids_in.at[sender], ids_send.at[s], ids_recv.at[sender], members[s])

    def field_halo(down):
        tile, target, device = (LINE, 0, below) if down else (1, LINE + 1, above)
        side = 0 if down else 1
        return remote(field_in.at[tile], field_in.at[target], fhalo_send.at[side], fhalo_recv.at[side], device)

    for s in range(LINE):
        field_into(s, place).start()
    for s in range(LINE):
        ids_into(s, place).start()
    for k in range(AHEAD):
        for s in range(LINE):
            into(k, s, place).start()

    def root_phase(p, carry):
        square = sigma[p] * sigma[p]
        for slot in range(SLOTS):
            depth = fields[pl.ds(2 * BLOCKS + ids_here[slot], 1), :]
            root[p, slot] = 1.0 / jnp.sqrt(wave_number(square, jnp.broadcast_to(depth, (8, LANES))))
        return carry

    lax.fori_loop(0, PHASES, root_phase, 0)

    for i in range(LINE):
        field_into(i, i).wait_recv()
    field_halo(True).start()
    field_halo(False).start()
    for i in range(LINE):
        ids_into(i, i).wait_recv()
    ids_copy = pltpu.make_async_copy(ids_in, ids_near, local_sem)
    ids_copy.start()
    ids_copy.wait()
    field_halo(True).wait_recv()
    field_halo(False).wait_recv()

    first_line = jnp.where(line == 0, 0.0, 1.0)
    last_line = jnp.where(line == lines - 1, 0.0, 1.0)

    def row_kept(tile):
        return jnp.where(tile == 0, first_line, jnp.where(tile == LINE + 1, last_line, 1.0))

    lane = lax.broadcasted_iota(jnp.int32, (8, 4 * LANES), 1)
    at_start = lane == 0
    at_end = lane == 4 * LANES - 1

    def shift_left(x):
        return jnp.where(at_end, 0.0, pltpu.roll(x, 4 * LANES - 1, 1))

    def field_row(tile, r, which):
        rows = [field_in[tile, pl.ds(which * BLOCKS + ct * 4 + r, 1), :] for ct in range(4)]
        return jnp.broadcast_to(jnp.concatenate(rows, axis=1), (8, 4 * LANES))

    def table_row(row, carry):
        tile, r = row // 4, lax.rem(row, 4)
        kept = row_kept(tile)
        cur_rows[row] = field_row(tile, r, 0) * (0.5 * STEP_RATIO * kept)
        across = field_row(tile, r, 1) * (0.5 * STEP_RATIO * kept)
        cur_cols[row] = across + shift_left(across)
        cur_cols_left[row] = across[:, :LANES]
        sea[row] = field_row(tile, r, 3) * kept
        depth = field_row(tile, r, 2)
        def one_phase(p, inner):
            sig = wide(sigma[p])
            wavenum = wave_number(sig * sig, depth)
            product = wavenum * depth
            damping = jnp.exp(-2.0 * product)
            shallow = 4.0 * product * damping / (1.0 - damping * damping)
            speed = (0.25 * STEP_RATIO * kept) * (sig / wavenum) * (1.0 + shallow)
            cg[row, p] = speed
            cg_cols[row, p] = speed + shift_left(speed)
            return inner
        lax.fori_loop(0, PHASES, one_phase, 0)
        return carry

    lax.fori_loop(0, 4 * TILES, table_row, 0)

    def face_row(row, carry):
        def one_phase(p, inner):
            cg_rows[row, p] = cg[row, p] + cg[row + 1, p]
            return inner
        lax.fori_loop(0, PHASES, one_phase, 0)
        cur_rows[row] = cur_rows[row] + cur_rows[row + 1]
        return carry

    lax.fori_loop(0, 4 * TILES - 1, face_row, 0)

    sub = lax.broadcasted_iota(jnp.int32, (8, 4 * LANES), 0)

    def advance(load, store, first, tiles, phase, cosine, sine):
        def face(row, near, far, slope_before, slope, slope_after):
            v = cg_rows[row, phase] * cosine + cur_rows[row]
            return face_flux(v, near, far, slope, slope_before, slope_after)

        rows = [load(first - 2 + j) for j in range(4)]
        slopes = [rows[j + 1] - rows[j] for j in range(3)]
        flux = face(first - 1, rows[1], rows[2], *slopes)

        def body(t, carry):
            near, far, slope_before, slope, flux_before = carry
            for r in range(4):
                row = first + 4 * t + r
                after = load(row + 2)
                slope_after = after - far
                flux = face(row, near, far, slope_before, slope, slope_after)
                mask = sea[row]
                x = (near - (flux - flux_before)) * mask
                right = shift_left(x)
                d = right - x
                d_before = jnp.where(at_start, x, pltpu.roll(d, 1, 1))
                d_after = shift_left(d)
                v = cg_cols[row, phase] * sine + cur_cols[row]
                across = face_flux(v, x, right, d, d_before, d_after)
                left = cg[row, phase, :, :LANES] * sine[:, :LANES] + cur_cols_left[row]
                x0, d0 = x[:, :LANES], d[:, :LANES]
                first_flux = jnp.minimum(left, 0.0) * (x0 - (0.5 + 0.5 * left) * minmod(d0, x0))
                before = jnp.where(at_start, wide(first_flux), pltpu.roll(across, 1, 1))
                store(t, r, (x - (across - before)) * mask)
                near, far, slope_before, slope, flux_before = far, after, slope, slope_after, flux
            return near, far, slope_before, slope, flux_before

        lax.fori_loop(0, tiles, body, (rows[2], rows[3], slopes[1], slopes[2], flux))

    def compute(k):
        def one_group(m, carry):
            group = STRIDE * place + CHUNK * k + m
            phase = lax.rem(group, PHASES)
            first_bin = other * (8 * GROUPS) + 8 * group
            d, f = first_bin // NF, lax.rem(first_bin, NF)
            later = sub >= NF - f
            cosine = jnp.where(later, trig[0, d + 1], trig[0, d])
            sine = jnp.where(later, trig[1, d + 1], trig[1, d])

            def load_first(row):
                tile, r = row // 4, lax.rem(row, 4)
                parts = [
                    arrived[k, tile, pl.ds(m * 8 * BLOCKS + ct * 4 + r, 8, stride=BLOCKS), :] for ct in range(4)
                ]
                return jnp.concatenate(parts, axis=1) * row_kept(tile)

            def store_first(t, r, value):
                moved[2 + 4 * t + r] = value

            def load_second(row):
                return moved[row]

            def store_second(t, r, value):
                for ct in range(4):
                    done[t * BLOCKS + ct * 4 + r] = value[:, ct * LANES : (ct + 1) * LANES]

            advance(load_first, store_first, 2, LINE + 1, phase, cosine, sine)
            advance(load_second, store_second, 4, LINE, phase, cosine, sine)
            for i in range(LINE):
                for slot in range(SLOTS):
                    packed[i, k, pl.ds((m * SLOTS + slot) * 8, 8), :] = done[i * BLOCKS + ids_near[i, 0, slot]]
            return carry

        lax.fori_loop(0, CHUNK, one_group, 0)

    def step(k, carry):
        @pl.when(k < CHUNKS)
        def _():
            for i in range(LINE):
                into(k, i, i).wait_recv()
            halo(k, True).start()
            halo(k, False).start()
            for s in range(LINE):
                into(k, s, place).wait_send()

        @pl.when(k + AHEAD < CHUNKS)
        def _():
            for s in range(LINE):
                into(k + AHEAD, s, place).start()

        @pl.when(k >= 1)
        def _():
            halo(k - 1, True).wait_recv()
            halo(k - 1, False).wait_recv()
            compute(k - 1)
            for i in range(LINE):
                back(k - 1, i, place).start()

        return carry

    lax.fori_loop(0, CHUNKS + 1, step, 0)

    def finish(k, carry):
        halo(k, True).wait_send()
        halo(k, False).wait_send()
        for i in range(LINE):
            back(k, i, place).wait_send()
        for i in range(LINE):
            back(k, i, i).wait_recv()
        return carry

    lax.fori_loop(0, CHUNKS, finish, 0)
    for s in range(LINE):
        field_into(s, place).wait_send()
        ids_into(s, place).wait_send()
    field_halo(True).wait_send()
    field_halo(False).wait_send()

    totals = [jnp.zeros((8, LANES), jnp.float32)] * (3 * SLOTS)
    for s in range(LINE):
        count = STRIDE if s < LINE - 1 else SLICE

        def add(g, carry, s=s):
            phase = lax.rem(STRIDE * s + g, PHASES)
            chunk, m = g // CHUNK, lax.rem(g, CHUNK)
            sig = sigma[phase]
            weight = sig * sig * (HALF_SPREAD * (2.0 * math.pi / ND))
            over = 1.0 / sig
            result = list(carry)
            for slot in range(SLOTS):
                energy = packed_out[s, chunk, pl.ds((m * SLOTS + slot) * 8, 8), :] * weight
                result[slot] += energy
                result[SLOTS + slot] += energy * over
                result[2 * SLOTS + slot] += energy * root[phase, slot]
            return tuple(result)

        totals = lax.fori_loop(0, count, add, tuple(totals))
    for q in range(3 * SLOTS):
        sums_mine[pl.ds(q, 1), :] = jnp.sum(totals[q], axis=0, keepdims=True)
    swap = remote(sums_mine, sums_other, sum_send, sum_recv, (space, other))
    swap.start()
    swap.wait()
    sums_out[...] = sums_mine[...] + sums_other[...]


def move(lines, spectrum, fields, ids, ids_here, trig, sigma):
    vmem = pl.BlockSpec(memory_space=pltpu.VMEM)
    smem = pl.BlockSpec(memory_space=pltpu.SMEM)
    rows = 4 * TILES
    f32 = jnp.float32
    dma = pltpu.SemaphoreType.DMA
    return pl.pallas_call(
        functools.partial(move_kernel, lines),
        out_shape=(
            jax.ShapeDtypeStruct((LINE, CHUNKS, PACK_ROWS, LANES), f32),
            jax.ShapeDtypeStruct((3 * SLOTS, LANES), f32),
        ),
        in_specs=[pl.BlockSpec(memory_space=pl.ANY), vmem, vmem, smem, smem, vmem],
        out_specs=(vmem, vmem),
        scratch_shapes=[
            pltpu.VMEM((CHUNKS, TILES, CHUNK_ROWS, LANES), f32),
            pltpu.VMEM((TILES, 4 * BLOCKS, LANES), f32),
            pltpu.VMEM((LINE, 8, LANES), jnp.int32),
            pltpu.SMEM((LINE, 8, LANES), jnp.int32),
            pltpu.VMEM((rows, PHASES, 8, 4 * LANES), f32),
            pltpu.VMEM((rows, PHASES, 8, 4 * LANES), f32),
            pltpu.VMEM((rows, PHASES, 8, 4 * LANES), f32),
            pltpu.VMEM((rows, 8, LANES), f32),
            pltpu.VMEM((rows, 8, 4 * LANES), f32),
            pltpu.VMEM((rows, 8, 4 * LANES), f32),
            pltpu.VMEM((rows, 8, 4 * LANES), f32),
            pltpu.VMEM((rows, 8, 4 * LANES), f32),
            pltpu.VMEM((LINE * BLOCKS, 8, LANES), f32),
            pltpu.VMEM((LINE, CHUNKS, PACK_ROWS, LANES), f32),
            pltpu.VMEM((PHASES, SLOTS, 8, LANES), f32),
            pltpu.VMEM((3 * SLOTS, LANES), f32),
            pltpu.VMEM((3 * SLOTS, LANES), f32),
            dma((CHUNKS, LINE)),
            dma((CHUNKS, LINE)),
            dma((CHUNKS, 2)),
            dma((CHUNKS, 2)),
            dma((CHUNKS, LINE)),
            dma((CHUNKS, LINE)),
            dma((LINE,)),
            dma((LINE,)),
            dma((2,)),
            dma((2,)),
            dma((LINE,)),
            dma((LINE,)),
            dma,
            dma,
            dma,
        ],
        compiler_params=pltpu.CompilerParams(
            collective_id=0, has_side_effects=True, vmem_limit_bytes=56 * 1024 * 1024
        ),
        cost_estimate=pl.CostEstimate(flops=250_000_000, bytes_accessed=16_000_000, transcendentals=1_000_000),
    )(spectrum, fields, ids, ids_here, trig, sigma)


def relax_kernel(packed, sums, fields, winds, ids, count, trig, sigma, out, number, brake):
    half = lax.axis_index("spec")
    j = pl.program_id(0)

    @pl.when(j == 0)
    def _():
        def tables(p, carry):
            sig = sigma[p]
            for slot in range(SLOTS):
                depth = jnp.broadcast_to(fields[pl.ds(2 * BLOCKS + ids[slot], 1), :], (8, LANES))
                wavenum = wave_number(sig * sig, depth)
                total = sums[pl.ds(slot, 1), :]
                mean_sigma = (total + EPSILON) / (sums[pl.ds(SLOTS + slot, 1), :] + EPSILON)
                ratio = (total + EPSILON) / (sums[pl.ds(2 * SLOTS + slot, 1), :] + EPSILON)
                mean_wavenum = ratio * ratio
                steep = total * mean_wavenum * mean_wavenum * (1.0 / STEEP_REF)
                rate = (SOURCE_STEP * DECAY_COEF) * mean_sigma * (wavenum / mean_wavenum) * (steep * steep)
                number[p, slot] = wavenum / sig
                brake[p, slot] = 1.0 / (1.0 + rate)
            return carry

        lax.fori_loop(0, PHASES, tables, 0)

    sub = lax.broadcasted_iota(jnp.int32, (8, LANES), 0)
    out[...] = jnp.zeros(out.shape, jnp.float32)
    for q in range(PHASES):
        group = PHASES * j + q
        first_bin = half * (8 * GROUPS) + 8 * group
        d, f = first_bin // NF, lax.rem(first_bin, NF)
        later = sub >= NF - f
        cosine = jnp.where(later, trig[0, d + 1], trig[0, d])
        sine = jnp.where(later, trig[1, d + 1], trig[1, d])
        s = jnp.minimum(group // STRIDE, LINE - 1)
        inside = group - STRIDE * s
        chunk, m = inside // CHUNK, lax.rem(inside, CHUNK)
        gain = sigma[q] * (SOURCE_STEP * INPUT_COEF)
        for slot in range(SLOTS):

            @pl.when(slot < count[0])
            def _(slot=slot):
                blk = ids[slot]
                along = winds[pl.ds(blk, 1), :] * cosine + winds[pl.ds(BLOCKS + blk, 1), :] * sine
                growth = gain * jnp.maximum(along * number[q, slot] - 1.0, 0.0)
                value = packed[s, chunk, pl.ds((m * SLOTS + slot) * 8, 8), :]
                out[pl.ds(q * 8 * BLOCKS + blk, 8, stride=BLOCKS), :] = (
                    value * (1.0 + growth) * brake[q, slot]
                )


def relax(packed, sums, fields, winds, ids, count, trig, sigma):
    vmem = pl.BlockSpec(memory_space=pltpu.VMEM)
    smem = pl.BlockSpec(memory_space=pltpu.SMEM)
    span = PHASES * 8 * BLOCKS
    return pl.pallas_call(
        relax_kernel,
        grid=(GROUPS // PHASES,),
        out_shape=jax.ShapeDtypeStruct((GROUPS * 8 * BLOCKS, LANES), jnp.float32),
        in_specs=[vmem, vmem, vmem, vmem, smem, smem, smem, vmem],
        out_specs=pl.BlockSpec((span, LANES), lambda j: (j, 0)),
        scratch_shapes=[
            pltpu.VMEM((PHASES, SLOTS, 8, LANES), jnp.float32),
            pltpu.VMEM((PHASES, SLOTS, 8, LANES), jnp.float32),
        ],
        compiler_params=pltpu.CompilerParams(vmem_limit_bytes=32 * 1024 * 1024),
        cost_estimate=pl.CostEstimate(flops=7_000_000, bytes_accessed=8_000_000, transcendentals=10_000),
    )(packed, sums, fields, winds, ids, count, trig, sigma)


def tile_rows(array):
    split = array.reshape(array.shape[:-1] + (4, LANES))
    return jnp.swapaxes(split, -3, -2).reshape(-1, LANES)


def on_device(lines, spectrum, current, depth, wind, sea_blocks):
    flags = sea_blocks.T.reshape(BLOCKS)
    rank = jnp.cumsum(flags) - 1
    count = jnp.sum(flags)
    block = jnp.arange(BLOCKS, dtype=jnp.int32)
    slots = jnp.arange(SLOTS, dtype=jnp.int32)
    chosen = (rank[None, :] == slots[:, None]) & (flags[None, :] > 0)
    ids = jnp.sum(jnp.where(chosen, block[None, :], 0), axis=1).astype(jnp.int32)
    ids_wide = jnp.zeros((8, LANES), jnp.int32).at[0, :SLOTS].set(ids)
    mask = jnp.broadcast_to(flags.astype(jnp.float32)[:, None], (BLOCKS, LANES))
    fields = jnp.concatenate([tile_rows(current), tile_rows(depth), mask], axis=0)
    angle = np.arange(ND + 1) * (2.0 * math.pi / ND)
    trig = jnp.asarray(np.stack([np.cos(angle), np.sin(angle)]).astype(np.float32))
    sigma = jnp.asarray(phase_table(sigma_values()))
    packed, sums = move(lines, tile_rows(spectrum), fields, ids_wide, ids, trig, sigma)
    out = relax(packed, sums, fields, tile_rows(wind), ids, count.reshape(1).astype(jnp.int32), trig, sigma)
    return jnp.swapaxes(out.reshape(-1, 4, 4, LANES), 1, 2).reshape(spectrum.shape)


def solution(mesh):
    placed = (
        P("spec", "space", None),
        P(None, "space", None),
        P("space", None),
        P(None, "space", None),
        P("space", None),
    )
    return jax.shard_map(
        functools.partial(on_device, mesh.shape["space"] // LINE),
        mesh=mesh,
        in_specs=placed,
        out_specs=P("spec", "space", None),
        check_vma=False,
    )
```

time: 626 us -> 155 us (0.25); the launches traced: 616 us -> 154 us
  other arithmetic: 316 us -> 3.82 us
  waiting for transfers between devices: 160 us -> 0 us
  Pallas kernels: 0 us -> 145 us
  blocking collectives: 63.3 us -> 0 us
  local copies, waits for them, and re-layouts: 54.5 us -> 5 us
  starting transfers between devices: 20.5 us -> 0 us
    mul x15 -> x0, other arithmetic: 179 us -> none  [the longest x4 116 us: advect_axis(): fluxes = face_speed * jnp.where(face_speed >= 0.0, face_up, face_down)]
    pallas_call x0 -> x2, Pallas kernels: none -> 145 us  [the longest x1 132 us: move(): pl.pallas_call(functools.partial(move_kernel, lines), out_shape=(jax.Shap...]
    ppermute x4 -> x0, waiting for transfers between devices: 102 us -> none  [the longest x2 53.6 us: with_halo(): before = lax.ppermute(last, axis, up)]
    all_to_all x1 -> x0, blocking collectives: 63.3 us -> none  [on_device(): lax.all_to_all(relaxed_here.reshape(ND * NF, point_blocks, 128), 'spec',...]
    all_to_all x1 -> x0, waiting for transfers between devices: 58.6 us -> none  [on_device(): lax.all_to_all(flat, 'spec', split_axis=1, concat_axis=0, tiled=True)]
    concatenate x4 -> x1, other arithmetic: 46.3 us -> 1.42 us  [on_device(): jnp.concatenate([tile_rows(current), tile_rows(depth), mask], axis=0)]
    div x2 -> x0, other arithmetic: 37.2 us -> none  [the longest x1 37.2 us: apply_rates(): spectra * (1.0 + SOURCE_STEP * growth) / (1.0 + SOURCE_STEP * decay_rate)]
    sub x4 -> x1, other arithmetic: 30.3 us -> 0.12 us  [on_device(): rank = jnp.cumsum(flags) - 1]
  transfers between devices with their start and end apart: 5 -> 0, of which waited for: 5 -> 0; matrix products, arithmetic and copies ran while one was open for 2% -> 0% of each run, Pallas kernels for 0% -> 0%
where the time goes in v1:
time: 155 us; the launch traced here: 154 us
  Pallas kernels  145 us (94%)
  local copies, waits for them, and re-layouts  5 us (3%)
  other arithmetic  3.82 us (2%)
    pallas_call x1, Pallas kernels, move(): pl.pallas_call(functools.partial(move_kernel, lines), out_shape=(jax.Shap...  132 us
    pallas_call x1, Pallas kernels, relax(): pl.pallas_call(relax_kernel, grid=(GROUPS // PHASES,), out_shape=jax.Shap...  13.5 us
    unnamed x16, local copies, waits for them, and re-layouts  3.1 us

profile of v1, /device:TPU:4, one launch (start us, length us, event | category | flops | bytes accessed | tf_op | source)
XLA Modules:
  0.0 154.1 jit_solution(3677905439332090819)
XLA Ops:
  0.0 0.0 copy-start.2
  0.0 0.0 copy-start.7
  0.0 0.0 copy-start.3
  0.0 0.7 broadcast_compare_fusion
  0.7 0.1 copy.32
  0.8 0.1 gt.12
  0.9 0.8 copy.30
  1.7 1.4 fusion.1
  3.1 0.1 copy.29
  3.2 0.1 reshape.122
  3.3 0.1 pad.7.clone
  3.4 0.1 reshape.120
  3.5 0.1 add_reduce_fusion
  3.6 0.1 select_reduce_fusion.ids_here.ids
  3.7 0.0 copy-start.5
  3.7 0.6 scatter.4.ids
  4.3 1.4 maximum_maximum_fusion.fields
  5.7 0.0 copy-done.5
  5.7 0.0 copy-start.1
  5.7 131.7 %shard_map.73 = (f32[4,7,192,128]{3,2,1,0:T(8,128)}, f32[24,128]{1,0:T(8,128)}) custom-call(f32[10368,128]{1,0:T(8,128)} %bitcast.32, f32[64,128]{1,0:T(8,128)} %maximum_maximum_fusion.fields, s32[8,128]{1,0:T(8,128)} %scatter.4.ids, s32[8]{0:T(128)} %copy-done.5, f32[2,37]{1,0:T(2,128)} %constant.39.clone.trig, f32[9,8,128]{2,1,0:T(8,128)} %constant.40.clone.sigma), custom_call_target="tpu_custom_call" | custom-call | flops 250000000 | bytes 16000000 | tf_op jit(solution)/shard_map/pallas_call | solution.py:395
  137.5 0.0 copy-done.2
  137.5 0.0 copy-done.7
  137.5 0.0 copy-done.3
  137.5 0.0 copy-done.1
  137.5 0.0 copy-start
  137.5 1.8 %copy-done = f32[4,7,192,128]{3,2,1,0:T(8,128)S(1)} copy-done((f32[4,7,192,128]{3,2,1,0:T(8,128)S(1)}, f32[4,7,192,128]{3,2,1,0:T(8,128)}, u32[]{:S(2)}) %copy-start) | copy-done | bytes 2752536
  139.3 0.0 copy-start.4
  139.3 0.7 copy-done.4
  140.0 0.0 copy-start.6
  140.0 0.6 copy-done.6
  140.6 13.5 %shard_map.74 = f32[10368,128]{1,0:T(8,128)} custom-call(f32[4,7,192,128]{3,2,1,0:T(8,128)S(1)} %copy-done, f32[24,128]{1,0:T(8,128)S(1)} %copy-done.4, f32[64,128]{1,0:T(8,128)S(1)} %copy-done.1, f32[32,128]{1,0:T(8,128)S(1)} %bitcast.30, s32[8]{0:T(128)S(1)} %copy-done.6, s32[1]{0:T(128)} %bitcast.14.count, f32[2,37]{1,0:T(2,128)S(1)} %copy-done.7, ...), custom_call_target="tpu_custom_call" | custom-call | flops 7000000 | bytes 8000000 | tf_op jit(solution)/shard_map/pallas_call | solution.py:497
  (1 shorter events, 0.0 us)
Async XLA Ops:
  0.0 137.5 %copy-start.2 = (f32[9,8,128]{2,1,0:T(8,128)S(1)}, f32[9,8,128]{2,1,0:T(8,128)}, u32[]{:S(2)}) copy-start(f32[9,8,128]{2,1,0:T(8,128)} %constant.40.clone.sigma) | copy-start | bytes 110596
  0.0 137.5 %copy-start.7 = (f32[2,37]{1,0:T(2,128)S(1)}, f32[2,37]{1,0:T(2,128)}, u32[]{:S(2)}) copy-start(f32[2,37]{1,0:T(2,128)} %constant.39.clone.trig) | copy-start | bytes 892
  0.0 137.5 %copy-start.3 = (f32[2,4,512]{2,1,0:T(4,128)S(1)}, f32[2,4,512]{2,1,0:T(4,128)}, u32[]{:S(2)}) copy-start(f32[2,4,512]{2,1,0:T(4,128)} %param.12) | copy-start | bytes 49156
  3.7 2.0 %copy-start.5 = (s32[8]{0:T(128)}, s32[8]{0:T(128)S(1)}, u32[]{:S(2)}) copy-start(s32[8]{0:T(128)S(1)} %select_reduce_fusion.ids_here.ids) | copy-start | bytes 100
  5.7 131.7 %copy-start.1 = (f32[64,128]{1,0:T(8,128)S(1)}, f32[64,128]{1,0:T(8,128)}, u32[]{:S(2)}) copy-start(f32[64,128]{1,0:T(8,128)} %maximum_maximum_fusion.fields) | copy-start | bytes 98308
  137.5 1.8 %copy-start = (f32[4,7,192,128]{3,2,1,0:T(8,128)S(1)}, f32[4,7,192,128]{3,2,1,0:T(8,128)}, u32[]{:S(2)}) copy-start(f32[4,7,192,128]{3,2,1,0:T(8,128)} %get-tuple-element.19.packed) | copy-start | bytes 8257540
  139.3 0.7 copy-start.4
  140.0 0.6 copy-start.6

commit v2 on v1

v2 whole, which is shorter than its diff:
```python
import functools
import math

import jax
import jax.numpy as jnp
import numpy as np
from jax import lax
from jax.experimental import pallas as pl
from jax.experimental.pallas import tpu as pltpu
from jax.sharding import PartitionSpec as P

MESH = pl.DeviceIdType.MESH
ND = 36
NF = 36
GRAVITY = 9.81
SIGMA_LOW = 2.0 * math.pi * 0.035
LOG_RATIO = math.log(1.1)
HALF_SPREAD = 0.5 * (1.1 - 1.0 / 1.1)
STEP_RATIO = 140.0 / 4600.0
SOURCE_STEP = 280.0
INPUT_COEF = 0.0002
DECAY_COEF = 0.002
STEEP_REF = 600.0
EPSILON = 1e-06

LINE = 4
LANES = 128
SLOTS = 8
GROUPS = 81
SLICE = 20
CHUNKS = ((0, 3), (3, 4), (7, 4), (11, 4), (15, 3), (18, 2), (20, 1))
LAST = len(CHUNKS) - 1
AHEAD = 4
PHASES = 9
TILES = LINE + 2
BLOCKS = 16
GROUP_ROWS = 8 * BLOCKS
PACK_ROWS = 8 * SLOTS
ROWS = 4 * TILES


def phase_tables():
    sigma = SIGMA_LOW * np.exp(np.arange(NF, dtype=np.float64) * LOG_RATIO)
    weight = sigma * sigma * HALF_SPREAD * (2.0 * math.pi / ND)
    index = (np.arange(PHASES)[:, None] * 8 + np.arange(8)[None, :]) % NF
    table = np.stack([sigma, weight, weight / sigma])[:, index].astype(np.float32)
    return np.broadcast_to(table[..., None], table.shape + (LANES,)).copy()


def columns(x):
    return [x[:, ct * LANES : (ct + 1) * LANES] for ct in range(4)]


def each(function, *lists):
    return [function(*parts) for parts in zip(*lists)]


def wave_number(square, depth):
    return square * (1.0 / GRAVITY) / jnp.sqrt(jnp.tanh(square * depth * (1.0 / GRAVITY)))


def face_flux(v, half, near, far, slope, slope_before, slope_after):
    up = v >= 0.0
    other_slope = jnp.where(up, slope_before, slope_after)
    limited = jnp.maximum(jnp.minimum(other_slope, jnp.maximum(slope, 0.0)), jnp.minimum(slope, 0.0))
    return v * (jnp.where(up, near, far) + half * limited)


def half_of(v):
    return jnp.where(v >= 0.0, 0.5, -0.5) - 0.5 * v


def bin_trig(trig, first_bin):
    d, f = first_bin // NF, lax.rem(first_bin, NF)
    later = lax.broadcasted_iota(jnp.int32, (8, LANES), 0) >= NF - f
    return f, jnp.where(later, trig[0, d + 1], trig[0, d]), jnp.where(later, trig[1, d + 1], trig[1, d])


def move_kernel(
    lines,
    spectrum,
    current,
    depth_here,
    flags,
    trig,
    tables,
    packed_out,
    sums_out,
    fields,
    ids,
    ids_here,
    arrived,
    field_in,
    ids_in,
    ids_near,
    cg,
    cg_rows,
    cg_cols,
    cur_rows,
    cur_cols,
    cur_left,
    sea,
    row_v,
    row_half,
    col_v,
    col_half,
    left_v,
    left_half,
    moved,
    done,
    packed,
    returned,
    root,
    sums_mine,
    sums_other,
    in_send,
    in_recv,
    halo_send,
    halo_recv,
    back_send,
    back_recv,
    field_send,
    field_recv,
    fhalo_send,
    fhalo_recv,
    ids_send,
    ids_recv,
    sum_send,
    sum_recv,
    local_sem,
):
    space = lax.axis_index("space")
    half = lax.axis_index("spec")
    other = 1 - half
    line = space // LINE
    place = lax.rem(space, LINE)
    above = (lax.rem(line + lines - 1, lines) * LINE + place, half)
    below = (lax.rem(line + 1, lines) * LINE + place, half)
    members = [(line * LINE + s, other) for s in range(LINE)]
    longer = place == LINE - 1

    barrier = pltpu.get_barrier_semaphore()
    for peer in members + [above, below]:
        pl.semaphore_signal(barrier, inc=1, device_id=peer, device_id_type=MESH)

    lane = lax.broadcasted_iota(jnp.int32, (8, LANES), 1)
    fields[: 2 * BLOCKS] = current[...]
    fields[2 * BLOCKS : 3 * BLOCKS] = depth_here[...]
    numbers = jnp.zeros((8, LANES), jnp.int32)
    found = jnp.int32(0)
    for blk in range(BLOCKS):
        flag = flags[blk % 4, blk // 4]
        fields[3 * BLOCKS + blk : 3 * BLOCKS + blk + 1] = jnp.full((1, LANES), flag.astype(jnp.float32))
        numbers = jnp.where(lane == jnp.where(flag > 0, found, -1), blk, numbers)
        found = found + flag
    ids[...] = numbers
    pl.semaphore_wait(barrier, LINE + 2)

    def remote(src, dst, send, recv, device):
        return pltpu.make_async_remote_copy(
            src_ref=src, dst_ref=dst, send_sem=send, recv_sem=recv, device_id=device, device_id_type=MESH
        )

    def into(c, s, sender):
        first, count = CHUNKS[c]
        return remote(
            spectrum.at[pl.ds((SLICE * s + first) * GROUP_ROWS, count * GROUP_ROWS)],
            arrived.at[1 + sender, pl.ds(first * GROUP_ROWS, count * GROUP_ROWS)],
            in_send.at[c, s],
            in_recv.at[c, sender],
            members[s],
        )

    def halo(c, down):
        first, count = CHUNKS[c]
        part = pl.ds(first * GROUP_ROWS, count * GROUP_ROWS)
        tile, target, device = (LINE, 0, below) if down else (1, LINE + 1, above)
        side = 0 if down else 1
        return remote(
            arrived.at[tile, part], arrived.at[target, part], halo_send.at[c, side], halo_recv.at[c, side], device
        )

    def back(c, i, sender):
        first, count = CHUNKS[c]
        start = pl.multiple_of((SLICE * sender + first) * PACK_ROWS, 8)
        return remote(
            packed.at[i, pl.ds(first * PACK_ROWS, count * PACK_ROWS)],
            returned.at[pl.ds(start, count * PACK_ROWS)],
            back_send.at[c, i],
            back_recv.at[c, sender],
            members[i],
        )

    def field_into(s, sender):
        return remote(fields, field_in.at[1 + sender], field_send.at[s], field_recv.at[sender], members[s])

    def ids_into(s, sender):
        return remote(ids, ids_in.at[sender], ids_send.at[s], ids_recv.at[sender], members[s])

    def field_halo(down):
        tile, target, device = (LINE, 0, below) if down else (1, LINE + 1, above)
        side = 0 if down else 1
        return remote(field_in.at[tile], field_in.at[target], fhalo_send.at[side], fhalo_recv.at[side], device)

    def slices(c):
        return range(LINE) if c < LAST else (LINE - 1,)

    def send_in(c):
        for s in slices(c):
            into(c, s, place).start()

    for s in range(LINE):
        field_into(s, place).start()
    for s in range(LINE):
        ids_into(s, place).start()
    for c in range(AHEAD):
        send_in(c)

    ids_copy = pltpu.make_async_copy(ids, ids_here, local_sem)
    ids_copy.start()
    ids_copy.wait()

    def root_phase(p, carry):
        square = tables[0, p] * tables[0, p]
        for slot in range(SLOTS):
            depth = fields[pl.ds(2 * BLOCKS + ids_here[0, slot], 1), :]
            root[p, slot] = tables[1, p] / jnp.sqrt(wave_number(square, jnp.broadcast_to(depth, (8, LANES))))
        return carry

    lax.fori_loop(0, PHASES, root_phase, 0)

    for i in range(LINE):
        field_into(i, i).wait_recv()
    field_halo(True).start()
    field_halo(False).start()
    for i in range(LINE):
        ids_into(i, i).wait_recv()
    near_copy = pltpu.make_async_copy(ids_in, ids_near, local_sem)
    near_copy.start()
    near_copy.wait()
    field_halo(True).wait_recv()
    field_halo(False).wait_recv()

    first_line = jnp.where(line == 0, 0.0, 1.0)
    last_line = jnp.where(line == lines - 1, 0.0, 1.0)
    at_start = lane == 0
    at_end = lane == LANES - 1

    def shift_left(parts):
        turned = [pltpu.roll(part, LANES - 1, 1) for part in parts] + [jnp.zeros((8, LANES), jnp.float32)]
        return [jnp.where(at_end, turned[ct + 1], turned[ct]) for ct in range(4)]

    def shift_right(parts, first):
        turned = [first] + [pltpu.roll(part, 1, 1) for part in parts]
        return [jnp.where(at_start, turned[ct], turned[ct + 1]) for ct in range(4)]

    def table_row(row, carry):
        tile, r = row // 4, lax.rem(row, 4)
        kept = jnp.where(tile == 0, first_line, jnp.where(tile == LINE + 1, last_line, 1.0))
        scale = 0.5 * STEP_RATIO * kept

        def field_row(which, ct):
            return jnp.broadcast_to(field_in[tile, pl.ds(which * BLOCKS + ct * 4 + r, 1), :], (8, LANES))

        across = [field_row(1, ct) * scale for ct in range(4)]
        cur_left[row] = across[0]
        faces = each(jnp.add, across, shift_left(across))
        for ct in range(4):
            cur_rows[row, ct] = field_row(0, ct) * scale
            cur_cols[row, ct] = faces[ct]
            sea[row, ct] = field_row(3, ct) * kept
        depths = [field_row(2, ct) for ct in range(4)]
        for p in range(5):
            sig = tables[0, p]
            speeds = []
            for ct in range(4):
                wavenum = wave_number(sig * sig, depths[ct])
                product = wavenum * depths[ct]
                damping = jnp.exp(-2.0 * product)
                shallow = 4.0 * product * damping / (1.0 - damping * damping)
                speeds.append((0.5 * scale) * (sig / wavenum) * (1.0 + shallow))
            faces = each(jnp.add, speeds, shift_left(speeds))
            for ct in range(4):
                cg[row, ct, 8 * p : 8 * p + 8] = speeds[ct]
                cg_cols[row, ct, 8 * p : 8 * p + 8] = faces[ct]
        return carry

    def face_row(row, carry):
        cg_rows[row] = cg[row] + cg[row + 1]
        cur_rows[row] = cur_rows[row] + cur_rows[row + 1]
        return carry

    def take_in(c):
        for i in range(LINE):
            into(c, i if c < LAST else LINE - 1, i).wait_recv()
        halo(c, True).start()
        halo(c, False).start()

    def send_more(c):
        for s in slices(c):
            into(c, s, place).wait_send()
        if c + AHEAD < LAST:
            send_in(c + AHEAD)
            if c + AHEAD == LAST - 1:
                send_in(LAST)

    lax.fori_loop(0, ROWS // 2, table_row, 0)
    take_in(0)
    send_more(0)
    lax.fori_loop(ROWS // 2, ROWS, table_row, 0)
    lax.fori_loop(0, ROWS - 1, face_row, 0)

    def advance(load, store, first, tiles, row_speed, col_speed, last_mask):
        rows = [load(first - 2 + j) for j in range(4)]
        slopes = [each(jnp.subtract, rows[j + 1], rows[j]) for j in range(3)]
        flux = each(face_flux, *row_speed(first - 1), rows[1], rows[2], slopes[1], slopes[0], slopes[2])

        def body(t, carry):
            near, far, slope_before, slope, flux_before = carry
            for r in range(4):
                row = first + 4 * t + r
                after = load(row + 2)
                slope_after = each(jnp.subtract, after, far)
                flux = each(face_flux, *row_speed(row), near, far, slope, slope_before, slope_after)
                mask = [sea[row, ct] for ct in range(4)]
                x = each(lambda n, a, b, m: (n - (a - b)) * m, near, flux, flux_before, mask)
                right = shift_left(x)
                d = each(jnp.subtract, right, x)
                v, half_v, edge_v, edge_half = col_speed(row)
                across = each(face_flux, v, half_v, x, right, d, shift_right(d, x[0]), shift_left(d))
                limited = jnp.maximum(jnp.minimum(d[0], jnp.maximum(x[0], 0.0)), jnp.minimum(x[0], 0.0))
                before = shift_right(across, edge_v * (x[0] - edge_half * limited))
                out = each(lambda n, a, b: n - (a - b), x, across, before)
                store(t, r, each(jnp.multiply, out, mask) if last_mask else out)
                near, far, slope_before, slope, flux_before = far, after, slope, slope_after, flux
            return near, far, slope_before, slope, flux_before

        lax.fori_loop(0, tiles, body, (rows[2], rows[3], slopes[1], slopes[2], flux))

    def one_group(group, carry):
        for c in range(1, LAST + 1):
            if c < LAST:

                @pl.when(group == CHUNKS[c - 1][0])
                def _(c=c):
                    take_in(c)
                    send_more(c)

            else:

                @pl.when((group == CHUNKS[c - 1][0]) & longer)
                def _(c=c):
                    take_in(c)

        for c in range(LAST + 1):

            @pl.when(group == CHUNKS[c][0])
            def _(c=c):
                halo(c, True).wait_recv()
                halo(c, False).wait_recv()
                first, count = CHUNKS[c]
                zeros = jnp.zeros((GROUP_ROWS, LANES), jnp.float32)

                @pl.when(line == 0)
                def _():
                    for q in range(count):
                        arrived[0, pl.ds((first + q) * GROUP_ROWS, GROUP_ROWS)] = zeros

                @pl.when(line == lines - 1)
                def _():
                    for q in range(count):
                        arrived[LINE + 1, pl.ds((first + q) * GROUP_ROWS, GROUP_ROWS)] = zeros

        f, cosine, sine = bin_trig(trig, other * (8 * GROUPS) + 8 * (SLICE * place + group))

        def load_first(row):
            tile, r = row // 4, lax.rem(row, 4)
            return [
                arrived[tile, pl.ds(group * GROUP_ROWS + ct * 4 + r, 8, stride=BLOCKS), :] for ct in range(4)
            ]

        def store_first(t, r, value):
            for ct in range(4):
                moved[2 + 4 * t + r, ct] = value[ct]

        def load_second(row):
            return [moved[row, ct] for ct in range(4)]

        def store_second(t, r, value):
            for ct in range(4):
                done[t * BLOCKS + ct * 4 + r] = value[ct]

        def row_first(row):
            v = [cg_rows[row, ct, pl.ds(f, 8), :] * cosine + cur_rows[row, ct] for ct in range(4)]
            halves = each(half_of, v)
            for ct in range(4):
                row_v[row, ct] = v[ct]
                row_half[row, ct] = halves[ct]
            return v, halves

        def col_first(row):
            v = [cg_cols[row, ct, pl.ds(f, 8), :] * sine + cur_cols[row, ct] for ct in range(4)]
            halves = each(half_of, v)
            for ct in range(4):
                col_v[row, ct] = v[ct]
                col_half[row, ct] = halves[ct]
            edge = cg[row, 0, pl.ds(f, 8), :] * sine + cur_left[row]
            edge_v, edge_half = jnp.minimum(edge, 0.0), 0.5 + 0.5 * edge
            left_v[row] = edge_v
            left_half[row] = edge_half
            return v, halves, edge_v, edge_half

        def row_again(row):
            return [row_v[row, ct] for ct in range(4)], [row_half[row, ct] for ct in range(4)]

        def col_again(row):
            v, halves = [col_v[row, ct] for ct in range(4)], [col_half[row, ct] for ct in range(4)]
            return v, halves, left_v[row], left_half[row]

        advance(load_first, store_first, 2, LINE + 1, row_first, col_first, True)
        advance(load_second, store_second, 4, LINE, row_again, col_again, False)
        for i in range(LINE):
            for slot in range(SLOTS):
                start = pl.multiple_of((group * SLOTS + slot) * 8, 8)
                packed[i, pl.ds(start, 8), :] = done[i * BLOCKS + ids_near[i, 0, slot]]

        for c in range(LAST + 1):

            @pl.when(group == CHUNKS[c][0] + CHUNKS[c][1] - 1)
            def _(c=c):
                for i in range(LINE):
                    back(c, i, place).start()

        return carry

    lax.fori_loop(0, jnp.where(longer, SLICE + 1, SLICE), one_group, 0)

    for c in range(LAST + 1):
        for s in slices(c):
            back(c, s, s).wait_recv()

    keep = pltpu.make_async_copy(returned, packed_out, local_sem)
    keep.start()

    def add(g, carry):
        phase = lax.rem(g, PHASES)
        weight, over = tables[1, phase], tables[2, phase]
        result = list(carry)
        for slot in range(SLOTS):
            start = pl.multiple_of((g * SLOTS + slot) * 8, 8)
            value = returned[pl.ds(start, 8), :]
            result[slot] += value * weight
            result[SLOTS + slot] += value * over
            result[2 * SLOTS + slot] += value * root[phase, slot]
        return tuple(result)

    totals = lax.fori_loop(0, GROUPS, add, (jnp.zeros((8, LANES), jnp.float32),) * (3 * SLOTS))
    for q in range(3 * SLOTS):
        sums_mine[pl.ds(q, 1), :] = jnp.sum(totals[q], axis=0, keepdims=True)
    swap = remote(sums_mine, sums_other, sum_send, sum_recv, (space, other))
    swap.start()

    for c in range(LAST):
        halo(c, True).wait_send()
        halo(c, False).wait_send()
        for i in range(LINE):
            back(c, i, place).wait_send()

    @pl.when(longer)
    def _():
        halo(LAST, True).wait_send()
        halo(LAST, False).wait_send()
        for i in range(LINE):
            back(LAST, i, place).wait_send()

    into(LAST, LINE - 1, place).wait_send()
    for s in range(LINE):
        field_into(s, place).wait_send()
        ids_into(s, place).wait_send()
    field_halo(True).wait_send()
    field_halo(False).wait_send()
    keep.wait()
    swap.wait()
    sums_out[...] = sums_mine[...] + sums_other[...]


def move(lines, spectrum, current, depth, flags, trig, tables):
    vmem = pl.BlockSpec(memory_space=pltpu.VMEM)
    smem = pl.BlockSpec(memory_space=pltpu.SMEM)
    hbm = pl.BlockSpec(memory_space=pl.ANY)
    f32 = jnp.float32
    dma = pltpu.SemaphoreType.DMA
    parts = len(CHUNKS)

    def tiles(*shape):
        return pltpu.VMEM(shape + (8, LANES), f32)

    return pl.pallas_call(
        functools.partial(move_kernel, lines),
        out_shape=(
            jax.ShapeDtypeStruct((GROUPS * PACK_ROWS, LANES), f32),
            jax.ShapeDtypeStruct((3 * SLOTS, LANES), f32),
        ),
        in_specs=[hbm, vmem, vmem, smem, smem, vmem],
        out_specs=(hbm, vmem),
        scratch_shapes=[
            pltpu.VMEM((4 * BLOCKS, LANES), f32),
            pltpu.VMEM((8, LANES), jnp.int32),
            pltpu.SMEM((8, LANES), jnp.int32),
            pltpu.VMEM((TILES, (SLICE + 1) * GROUP_ROWS, LANES), f32),
            pltpu.VMEM((TILES, 4 * BLOCKS, LANES), f32),
            pltpu.VMEM((LINE, 8, LANES), jnp.int32),
            pltpu.SMEM((LINE, 8, LANES), jnp.int32),
            pltpu.VMEM((ROWS, 4, 40, LANES), f32),
            pltpu.VMEM((ROWS, 4, 40, LANES), f32),
            pltpu.VMEM((ROWS, 4, 40, LANES), f32),
            tiles(ROWS, 4),
            tiles(ROWS, 4),
            tiles(ROWS),
            tiles(ROWS, 4),
            tiles(ROWS, 4),
            tiles(ROWS, 4),
            tiles(ROWS, 4),
            tiles(ROWS, 4),
            tiles(ROWS),
            tiles(ROWS),
            tiles(ROWS, 4),
            tiles(LINE * BLOCKS),
            pltpu.VMEM((LINE, (SLICE + 1) * PACK_ROWS, LANES), f32),
            pltpu.VMEM((GROUPS * PACK_ROWS, LANES), f32),
            tiles(PHASES, SLOTS),
            pltpu.VMEM((3 * SLOTS, LANES), f32),
            pltpu.VMEM((3 * SLOTS, LANES), f32),
            dma((parts, LINE)),
            dma((parts, LINE)),
            dma((parts, 2)),
            dma((parts, 2)),
            dma((parts, LINE)),
            dma((parts, LINE)),
            dma((LINE,)),
            dma((LINE,)),
            dma((2,)),
            dma((2,)),
            dma((LINE,)),
            dma((LINE,)),
            dma,
            dma,
            dma,
        ],
        compiler_params=pltpu.CompilerParams(
            collective_id=0, has_side_effects=True, vmem_limit_bytes=56 * 1024 * 1024
        ),
        cost_estimate=pl.CostEstimate(flops=250_000_000, bytes_accessed=16_000_000, transcendentals=1_000_000),
    )(spectrum, current, depth, flags, trig, tables)


def relax_kernel(packed, sums, depths, winds, flags, trig, tables, out, ids, gusts, number, brake):
    half = lax.axis_index("spec")
    j = pl.program_id(0)

    @pl.when(j == 0)
    def _():
        total = jnp.int32(0)
        for blk in range(BLOCKS):
            total = total + flags[blk % 4, blk // 4]
        found, dry = jnp.int32(0), total
        for blk in range(BLOCKS):
            flag = flags[blk % 4, blk // 4]
            ids[jnp.where(flag > 0, found, dry)] = blk
            found = found + flag
            dry = dry + 1 - flag
        for slot in range(SLOTS):
            blk = ids[slot]
            gusts[0, slot] = jnp.broadcast_to(winds[pl.ds(blk, 1), :], (8, LANES))
            gusts[1, slot] = jnp.broadcast_to(winds[pl.ds(BLOCKS + blk, 1), :], (8, LANES))
        rates = []
        for slot in range(SLOTS):
            total_here = sums[pl.ds(slot, 1), :]
            mean_sigma = (total_here + EPSILON) / (sums[pl.ds(SLOTS + slot, 1), :] + EPSILON)
            ratio = (total_here + EPSILON) / (sums[pl.ds(2 * SLOTS + slot, 1), :] + EPSILON)
            mean_wavenum = ratio * ratio
            steep = total_here * mean_wavenum * mean_wavenum * (1.0 / STEEP_REF)
            rates.append((SOURCE_STEP * DECAY_COEF) * mean_sigma / mean_wavenum * (steep * steep))

        def fill(p, carry):
            sig = tables[0, p]
            for slot in range(SLOTS):
                depth = jnp.broadcast_to(depths[pl.ds(ids[slot], 1), :], (8, LANES))
                wavenum = wave_number(sig * sig, depth)
                at_sea = jnp.where(slot < total, 1.0, 0.0)
                number[p, slot] = wavenum * (SOURCE_STEP * INPUT_COEF)
                brake[p, slot] = at_sea / (1.0 + rates[slot] * wavenum)
            return carry

        lax.fori_loop(0, PHASES, fill, 0)

    zeros = jnp.zeros((8, LANES), jnp.float32)
    for q in range(PHASES):
        f, cosine, sine = bin_trig(trig, half * (8 * GROUPS) + 8 * (PHASES * j + q))
        gain = tables[0, q] * (SOURCE_STEP * INPUT_COEF)
        for slot in range(SLOTS):
            along = gusts[0, slot] * cosine + gusts[1, slot] * sine
            growth = jnp.maximum(along * number[q, slot] - gain, 0.0)
            value = packed[pl.ds((q * SLOTS + slot) * 8, 8), :]
            out[pl.ds(q * GROUP_ROWS + ids[slot], 8, stride=BLOCKS), :] = value * (1.0 + growth) * brake[q, slot]
        for slot in range(SLOTS, BLOCKS):
            out[pl.ds(q * GROUP_ROWS + ids[slot], 8, stride=BLOCKS), :] = zeros


def relax(packed, sums, depth, wind, flags, trig, tables):
    vmem = pl.BlockSpec(memory_space=pltpu.VMEM)
    smem = pl.BlockSpec(memory_space=pltpu.SMEM)
    f32 = jnp.float32
    return pl.pallas_call(
        relax_kernel,
        grid=(GROUPS // PHASES,),
        out_shape=jax.ShapeDtypeStruct((GROUPS * GROUP_ROWS, LANES), f32),
        in_specs=[pl.BlockSpec((PHASES * PACK_ROWS, LANES), lambda j: (j, 0)), vmem, vmem, vmem, smem, smem, vmem],
        out_specs=pl.BlockSpec((PHASES * GROUP_ROWS, LANES), lambda j: (j, 0)),
        scratch_shapes=[
            pltpu.SMEM((BLOCKS,), jnp.int32),
            pltpu.VMEM((2, SLOTS, 8, LANES), f32),
            pltpu.VMEM((PHASES, SLOTS, 8, LANES), f32),
            pltpu.VMEM((PHASES, SLOTS, 8, LANES), f32),
        ],
        compiler_params=pltpu.CompilerParams(vmem_limit_bytes=32 * 1024 * 1024),
        cost_estimate=pl.CostEstimate(flops=7_000_000, bytes_accessed=8_000_000, transcendentals=10_000),
    )(packed, sums, depth, wind, flags, trig, tables)


def tile_rows(array):
    split = array.reshape(array.shape[:-1] + (4, LANES))
    return jnp.swapaxes(split, -3, -2).reshape(-1, LANES)


def on_device(lines, spectrum, current, depth, wind, sea_blocks):
    angle = np.arange(ND + 1) * (2.0 * math.pi / ND)
    trig = jnp.asarray(np.stack([np.cos(angle), np.sin(angle)]).astype(np.float32))
    tables = jnp.asarray(phase_tables())
    depth_rows = tile_rows(depth)
    packed, sums = move(lines, tile_rows(spectrum), tile_rows(current), depth_rows, sea_blocks, trig, tables)
    out = relax(packed, sums, depth_rows, tile_rows(wind), sea_blocks, trig, tables)
    return jnp.swapaxes(out.reshape(-1, 4, 4, LANES), 1, 2).reshape(spectrum.shape)


def solution(mesh):
    placed = (
        P("spec", "space", None),
        P(None, "space", None),
        P("space", None),
        P(None, "space", None),
        P("space", None),
    )
    return jax.shard_map(
        functools.partial(on_device, mesh.shape["space"] // LINE),
        mesh=mesh,
        in_specs=placed,
        out_specs=P("spec", "space", None),
        check_vma=False,
    )
```

time: 155 us -> 115 us (0.74)
  Pallas kernels: 145 us -> 111 us
  other arithmetic: 3.82 us -> 0 us
  local copies, waits for them, and re-layouts: 5 us -> 2.47 us
    pallas_call x1, Pallas kernels: 132 us -> 104 us  [move(): pl.pallas_call(functools.partial(move_kernel, lines), out_shape=(jax.Shap...]
    pallas_call x1, Pallas kernels: 13.5 us -> 6.58 us  [relax(): pl.pallas_call(relax_kernel, grid=(GROUPS // PHASES,), out_shape=jax.Shap...]
    unnamed x16 -> x14, local copies, waits for them, and re-layouts: 3.1 us -> 2.47 us
where the time goes in v2:
time: 115 us; the launch traced here: 113 us
  Pallas kernels  111 us (97%)
  local copies, waits for them, and re-layouts  2.47 us (2%)
    pallas_call x1, Pallas kernels, move(): pl.pallas_call(functools.partial(move_kernel, lines), out_shape=(jax.Shap...  104 us
    pallas_call x1, Pallas kernels, relax(): pl.pallas_call(relax_kernel, grid=(GROUPS // PHASES,), out_shape=jax.Shap...  6.58 us
    unnamed x14, local copies, waits for them, and re-layouts  2.47 us

profile of v2, /device:TPU:4, one launch (start us, length us, event | category | flops | bytes accessed | tf_op | source)
XLA Modules:
  0.0 113.4 jit_solution(16004376436166514335)
XLA Ops:
  0.0 0.0 copy-start.1
  0.0 0.0 copy-start.6
  0.0 0.0 copy-start.5
  0.0 0.0 copy-start.3
  0.0 0.0 copy-start.2
  0.0 104.3 %shard_map.73 = (f32[5184,128]{1,0:T(8,128)}, f32[24,128]{1,0:T(8,128)}) custom-call(f32[10368,128]{1,0:T(8,128)} %bitcast.28, f32[32,128]{1,0:T(8,128)} %bitcast.29, f32[16,128]{1,0:T(8,128)} %bitcast.25, s32[4,4]{1,0:T(4,128)} %flags.3, f32[2,37]{1,0:T(2,128)} %constant.4.clone.trig, f32[3,9,8,128]{3,2,1,0:T(8,128)} %constant.5.clone.tables), custom_call_target="tpu_custom_call" | custom-call | flops 250000000 | bytes 16000000 | tf_op jit(solution)/shard_map/pallas_call | solution.py:498
  104.3 0.0 copy-done.1
  104.3 0.0 copy-done.6
  104.3 0.0 copy-done.5
  104.3 0.0 copy-done.3
  104.4 0.0 copy-done.2
  104.4 0.0 copy-start
  104.4 1.7 %copy-done = f32[5184,128]{1,0:T(8,128)S(1)} copy-done((f32[5184,128]{1,0:T(8,128)S(1)}, f32[5184,128]{1,0:T(8,128)}, u32[]{:S(2)}) %copy-start) | copy-done | bytes 2654232
  106.1 0.0 copy-start.4
  106.1 0.7 copy-done.4
  106.8 6.6 %shard_map.74 = f32[10368,128]{1,0:T(8,128)} custom-call(f32[5184,128]{1,0:T(8,128)S(1)} %copy-done, f32[24,128]{1,0:T(8,128)S(1)} %copy-done.4, f32[16,128]{1,0:T(8,128)S(1)} %bitcast.26, f32[32,128]{1,0:T(8,128)S(1)} %bitcast.27, s32[4,4]{1,0:T(4,128)S(1)} %copy-done.5, f32[2,37]{1,0:T(2,128)S(1)} %copy-done.6, f32[3,9,8,128]{3,2,1,0:T(8,128)S(1)} %copy-done.1), custom_call_target="tpu_custom_call" | custom-call | flops 7000000 | bytes 8000000 | tf_op jit(solution)/shard_map/pallas_call | solution.py:614
Async XLA Ops:
  0.0 104.3 %copy-start.1 = (f32[3,9,8,128]{3,2,1,0:T(8,128)S(1)}, f32[3,9,8,128]{3,2,1,0:T(8,128)}, u32[]{:S(2)}) copy-start(f32[3,9,8,128]{3,2,1,0:T(8,128)} %constant.5.clone.tables) | copy-start | bytes 331780
  0.0 104.3 %copy-start.6 = (f32[2,37]{1,0:T(2,128)S(1)}, f32[2,37]{1,0:T(2,128)}, u32[]{:S(2)}) copy-start(f32[2,37]{1,0:T(2,128)} %constant.4.clone.trig) | copy-start | bytes 892
  0.0 104.3 %copy-start.5 = (s32[4,4]{1,0:T(4,128)S(1)}, s32[4,4]{1,0:T(4,128)}, u32[]{:S(2)}) copy-start(s32[4,4]{1,0:T(4,128)} %flags.3) | copy-start | bytes 196
  0.0 104.3 %copy-start.3 = (f32[2,4,512]{2,1,0:T(4,128)S(1)}, f32[2,4,512]{2,1,0:T(4,128)}, u32[]{:S(2)}) copy-start(f32[2,4,512]{2,1,0:T(4,128)} %param.10) | copy-start | bytes 49156
  0.0 104.3 %copy-start.2 = (f32[4,512]{1,0:T(4,128)S(1)}, f32[4,512]{1,0:T(4,128)}, u32[]{:S(2)}) copy-start(f32[4,512]{1,0:T(4,128)} %param.9) | copy-start | bytes 24580
  104.4 1.8 %copy-start = (f32[5184,128]{1,0:T(8,128)S(1)}, f32[5184,128]{1,0:T(8,128)}, u32[]{:S(2)}) copy-start(f32[5184,128]{1,0:T(8,128)} %get-tuple-element.7.packed) | copy-start | bytes 7962628
  106.1 0.7 copy-start.4

commit v3 on v2

--- a/solution.py
+++ b/solution.py
@@ -28,9 +28,9 @@
 SLOTS = 8
 GROUPS = 81
 SLICE = 20
-CHUNKS = ((0, 3), (3, 4), (7, 4), (11, 4), (15, 3), (18, 2), (20, 1))
+CHUNKS = ((0, 2), (2, 3), (5, 3), (8, 3), (11, 3), (14, 2), (16, 2), (18, 1), (19, 1), (20, 1))
 LAST = len(CHUNKS) - 1
-AHEAD = 4
+EARLY = 4
 PHASES = 9
 TILES = LINE + 2
 BLOCKS = 16
@@ -81,6 +81,7 @@
     spectrum,
     current,
     depth_here,
+    winds,
     flags,
     trig,
     tables,
@@ -111,6 +112,8 @@
     packed,
     returned,
     root,
+    number,
+    gusts,
     sums_mine,
     sums_other,
     in_send,
@@ -213,7 +216,10 @@
         field_into(s, place).start()
     for s in range(LINE):
         ids_into(s, place).start()
-    for c in range(AHEAD):
+    for c in range(EARLY):
+        send_in(c)
+    send_in(LAST)
+    for c in range(EARLY, LAST):
         send_in(c)
 
     ids_copy = pltpu.make_async_copy(ids, ids_here, local_sem)
@@ -224,8 +230,15 @@
         square = tables[0, p] * tables[0, p]
         for slot in range(SLOTS):
             depth = fields[pl.ds(2 * BLOCKS + ids_here[0, slot], 1), :]
-            root[p, slot] = tables[1, p] / jnp.sqrt(wave_number(square, jnp.broadcast_to(depth, (8, LANES))))
+            wavenum = wave_number(square, jnp.broadcast_to(depth, (8, LANES)))
+            root[p, slot] = tables[1, p] / jnp.sqrt(wavenum)
+            number[p, slot] = wavenum * (SOURCE_STEP * INPUT_COEF)
         return carry
+
+    for slot in range(SLOTS):
+        for part in range(2):
+            wind = winds[pl.ds(part * BLOCKS + ids_here[0, slot], 1), :]
+            gusts[part, slot] = jnp.broadcast_to(wind, (8, LANES))
 
     lax.fori_loop(0, PHASES, root_phase, 0)
 
@@ -296,17 +309,8 @@
         halo(c, True).start()
         halo(c, False).start()
 
-    def send_more(c):
-        for s in slices(c):
-            into(c, s, place).wait_send()
-        if c + AHEAD < LAST:
-            send_in(c + AHEAD)
-            if c + AHEAD == LAST - 1:
-                send_in(LAST)
-
     lax.fori_loop(0, ROWS // 2, table_row, 0)
     take_in(0)
-    send_more(0)
     lax.fori_loop(ROWS // 2, ROWS, table_row, 0)
     lax.fori_loop(0, ROWS - 1, face_row, 0)
 
@@ -344,7 +348,6 @@
                 @pl.when(group == CHUNKS[c - 1][0])
                 def _(c=c):
                     take_in(c)
-                    send_more(c)
 
             else:
 
@@ -435,26 +438,43 @@
 
     lax.fori_loop(0, jnp.where(longer, SLICE + 1, SLICE), one_group, 0)
 
+    for s in range(LINE):
+        field_into(s, place).wait_send()
+        ids_into(s, place).wait_send()
+    field_halo(True).wait_send()
+    field_halo(False).wait_send()
     for c in range(LAST + 1):
         for s in slices(c):
+            into(c, s, place).wait_send()
+
+    totals = (jnp.zeros((8, LANES), jnp.float32),) * (3 * SLOTS)
+    for c in (*range(EARLY), LAST, *range(EARLY, LAST)):
+        for s in slices(c):
             back(c, s, s).wait_recv()
 
+        def add(m, carry, c=c):
+            result = list(carry)
+            for s in slices(c):
+                g = SLICE * s + m
+                phase = lax.rem(g, PHASES)
+                weight, over = tables[1, phase], tables[2, phase]
+                gain = tables[0, phase] * (SOURCE_STEP * INPUT_COEF)
+                _, cosine, sine = bin_trig(trig, half * (8 * GROUPS) + 8 * g)
+                for slot in range(SLOTS):
+                    start = pl.multiple_of((g * SLOTS + slot) * 8, 8)
+                    value = returned[pl.ds(start, 8), :]
+                    result[slot] += value * weight
+                    result[SLOTS + slot] += value * over
+                    result[2 * SLOTS + slot] += value * root[phase, slot]
+                    along = gusts[0, slot] * cosine + gusts[1, slot] * sine
+                    growth = jnp.maximum(along * number[phase, slot] - gain, 0.0)
+                    returned[pl.ds(start, 8), :] = value * (1.0 + growth)
+            return tuple(result)
+
+        first, count = CHUNKS[c]
+        totals = lax.fori_loop(first, first + count, add, totals)
     keep = pltpu.make_async_copy(returned, packed_out, local_sem)
     keep.start()
-
-    def add(g, carry):
-        phase = lax.rem(g, PHASES)
-        weight, over = tables[1, phase], tables[2, phase]
-        result = list(carry)
-        for slot in range(SLOTS):
-            start = pl.multiple_of((g * SLOTS + slot) * 8, 8)
-            value = returned[pl.ds(start, 8), :]
-            result[slot] += value * weight
-            result[SLOTS + slot] += value * over
-            result[2 * SLOTS + slot] += value * root[phase, slot]
-        return tuple(result)
-
-    totals = lax.fori_loop(0, GROUPS, add, (jnp.zeros((8, LANES), jnp.float32),) * (3 * SLOTS))
     for q in range(3 * SLOTS):
         sums_mine[pl.ds(q, 1), :] = jnp.sum(totals[q], axis=0, keepdims=True)
     swap = remote(sums_mine, sums_other, sum_send, sum_recv, (space, other))
@@ -473,18 +493,12 @@
         for i in range(LINE):
             back(LAST, i, place).wait_send()
 
-    into(LAST, LINE - 1, place).wait_send()
-    for s in range(LINE):
-        field_into(s, place).wait_send()
-        ids_into(s, place).wait_send()
-    field_halo(True).wait_send()
-    field_halo(False).wait_send()
     keep.wait()
     swap.wait()
     sums_out[...] = sums_mine[...] + sums_other[...]
 
 
-def move(lines, spectrum, current, depth, flags, trig, tables):
+def move(lines, spectrum, current, depth, wind, flags, trig, tables):
     vmem = pl.BlockSpec(memory_space=pltpu.VMEM)
     smem = pl.BlockSpec(memory_space=pltpu.SMEM)
     hbm = pl.BlockSpec(memory_space=pl.ANY)
@@ -501,7 +515,7 @@
             jax.ShapeDtypeStruct((GROUPS * PACK_ROWS, LANES), f32),
             jax.ShapeDtypeStruct((3 * SLOTS, LANES), f32),
         ),
-        in_specs=[hbm, vmem, vmem, smem, smem, vmem],
+        in_specs=[hbm, vmem, vmem, vmem, smem, smem, vmem],
         out_specs=(hbm, vmem),
         scratch_shapes=[
             pltpu.VMEM((4 * BLOCKS, LANES), f32),
@@ -529,6 +543,8 @@
             pltpu.VMEM((LINE, (SLICE + 1) * PACK_ROWS, LANES), f32),
             pltpu.VMEM((GROUPS * PACK_ROWS, LANES), f32),
             tiles(PHASES, SLOTS),
+            tiles(PHASES, SLOTS),
+            tiles(2, SLOTS),
             pltpu.VMEM((3 * SLOTS, LANES), f32),
             pltpu.VMEM((3 * SLOTS, LANES), f32),
             dma((parts, LINE)),
@@ -551,81 +567,89 @@
             collective_id=0, has_side_effects=True, vmem_limit_bytes=56 * 1024 * 1024
         ),
         cost_estimate=pl.CostEstimate(flops=250_000_000, bytes_accessed=16_000_000, transcendentals=1_000_000),
-    )(spectrum, current, depth, flags, trig, tables)
-
-
-def relax_kernel(packed, sums, depths, winds, flags, trig, tables, out, ids, gusts, number, brake):
-    half = lax.axis_index("spec")
-    j = pl.program_id(0)
-
-    @pl.when(j == 0)
-    def _():
-        total = jnp.int32(0)
-        for blk in range(BLOCKS):
-            total = total + flags[blk % 4, blk // 4]
-        found, dry = jnp.int32(0), total
-        for blk in range(BLOCKS):
-            flag = flags[blk % 4, blk // 4]
-            ids[jnp.where(flag > 0, found, dry)] = blk
-            found = found + flag
-            dry = dry + 1 - flag
-        for slot in range(SLOTS):
-            blk = ids[slot]
-            gusts[0, slot] = jnp.broadcast_to(winds[pl.ds(blk, 1), :], (8, LANES))
-            gusts[1, slot] = jnp.broadcast_to(winds[pl.ds(BLOCKS + blk, 1), :], (8, LANES))
-        rates = []
-        for slot in range(SLOTS):
-            total_here = sums[pl.ds(slot, 1), :]
-            mean_sigma = (total_here + EPSILON) / (sums[pl.ds(SLOTS + slot, 1), :] + EPSILON)
-            ratio = (total_here + EPSILON) / (sums[pl.ds(2 * SLOTS + slot, 1), :] + EPSILON)
-            mean_wavenum = ratio * ratio
-            steep = total_here * mean_wavenum * mean_wavenum * (1.0 / STEEP_REF)
-            rates.append((SOURCE_STEP * DECAY_COEF) * mean_sigma / mean_wavenum * (steep * steep))
-
-        def fill(p, carry):
-            sig = tables[0, p]
+    )(spectrum, current, depth, wind, flags, trig, tables)
+
+
+def relax_kernel(packed, sums, depths, flags, tables, out, loaded, ids, brake, staged, in_sems, out_sems):
+    span_in, span_out = PHASES * PACK_ROWS, PHASES * GROUP_ROWS
+    steps = GROUPS // PHASES
+
+    def copy_in(j):
+        part = pl.ds(pl.multiple_of(j * span_in, 8), span_in)
+        return pltpu.make_async_copy(packed.at[part], loaded.at[part], in_sems.at[j])
+
+    def copy_out(j):
+        here = lax.rem(j, 2)
+        part = pl.ds(pl.multiple_of(j * span_out, 8), span_out)
+        return pltpu.make_async_copy(staged.at[here], out.at[part], out_sems.at[here])
+
+    for j in range(steps):
+        copy_in(j).start()
+
+    total = jnp.int32(0)
+    for blk in range(BLOCKS):
+        total = total + flags[blk % 4, blk // 4]
+    found, dry = jnp.int32(0), total
+    for blk in range(BLOCKS):
+        flag = flags[blk % 4, blk // 4]
+        ids[jnp.where(flag > 0, found, dry)] = blk
+        found = found + flag
+        dry = dry + 1 - flag
+    staged[...] = jnp.zeros(staged.shape, jnp.float32)
+    for slot in range(SLOTS):
+        here = sums[pl.ds(slot, 1), :]
+        mean_sigma = (here + EPSILON) / (sums[pl.ds(SLOTS + slot, 1), :] + EPSILON)
+        ratio = (here + EPSILON) / (sums[pl.ds(2 * SLOTS + slot, 1), :] + EPSILON)
+        mean_wavenum = ratio * ratio
+        steep = here * mean_wavenum * mean_wavenum * (1.0 / STEEP_REF)
+        rate = (SOURCE_STEP * DECAY_COEF) * mean_sigma / mean_wavenum * (steep * steep)
+        depth = jnp.broadcast_to(depths[pl.ds(ids[slot], 1), :], (8, LANES))
+        at_sea = jnp.where(slot < total, 1.0, 0.0)
+        for p in range(PHASES):
+            wavenum = wave_number(tables[0, p] * tables[0, p], depth)
+            brake[p, slot] = at_sea / (1.0 + rate * wavenum)
+
+    def step(j, carry):
+        @pl.when(j >= 2)
+        def _():
+            copy_out(j - 2).wait()
+
+        copy_in(j).wait()
+        here = lax.rem(j, 2)
+        for q in range(PHASES):
             for slot in range(SLOTS):
-                depth = jnp.broadcast_to(depths[pl.ds(ids[slot], 1), :], (8, LANES))
-                wavenum = wave_number(sig * sig, depth)
-                at_sea = jnp.where(slot < total, 1.0, 0.0)
-                number[p, slot] = wavenum * (SOURCE_STEP * INPUT_COEF)
-                brake[p, slot] = at_sea / (1.0 + rates[slot] * wavenum)
-            return carry
-
-        lax.fori_loop(0, PHASES, fill, 0)
-
-    zeros = jnp.zeros((8, LANES), jnp.float32)
-    for q in range(PHASES):
-        f, cosine, sine = bin_trig(trig, half * (8 * GROUPS) + 8 * (PHASES * j + q))
-        gain = tables[0, q] * (SOURCE_STEP * INPUT_COEF)
-        for slot in range(SLOTS):
-            along = gusts[0, slot] * cosine + gusts[1, slot] * sine
-            growth = jnp.maximum(along * number[q, slot] - gain, 0.0)
-            value = packed[pl.ds((q * SLOTS + slot) * 8, 8), :]
-            out[pl.ds(q * GROUP_ROWS + ids[slot], 8, stride=BLOCKS), :] = value * (1.0 + growth) * brake[q, slot]
-        for slot in range(SLOTS, BLOCKS):
-            out[pl.ds(q * GROUP_ROWS + ids[slot], 8, stride=BLOCKS), :] = zeros
-
-
-def relax(packed, sums, depth, wind, flags, trig, tables):
+                row = pl.multiple_of(j * span_in + (q * SLOTS + slot) * 8, 8)
+                place = pl.ds(q * GROUP_ROWS + ids[slot], 8, stride=BLOCKS)
+                staged[here, place, :] = loaded[pl.ds(row, 8), :] * brake[q, slot]
+        copy_out(j).start()
+        return carry
+
+    lax.fori_loop(0, steps, step, 0)
+    copy_out(steps - 2).wait()
+    copy_out(steps - 1).wait()
+
+
+def relax(packed, sums, depth, flags, tables):
     vmem = pl.BlockSpec(memory_space=pltpu.VMEM)
     smem = pl.BlockSpec(memory_space=pltpu.SMEM)
+    hbm = pl.BlockSpec(memory_space=pl.ANY)
     f32 = jnp.float32
     return pl.pallas_call(
         relax_kernel,
-        grid=(GROUPS // PHASES,),
         out_shape=jax.ShapeDtypeStruct((GROUPS * GROUP_ROWS, LANES), f32),
-        in_specs=[pl.BlockSpec((PHASES * PACK_ROWS, LANES), lambda j: (j, 0)), vmem, vmem, vmem, smem, smem, vmem],
-        out_specs=pl.BlockSpec((PHASES * GROUP_ROWS, LANES), lambda j: (j, 0)),
+        in_specs=[hbm, vmem, vmem, smem, vmem],
+        out_specs=hbm,
         scratch_shapes=[
+            pltpu.VMEM((GROUPS * PACK_ROWS, LANES), f32),
             pltpu.SMEM((BLOCKS,), jnp.int32),
-            pltpu.VMEM((2, SLOTS, 8, LANES), f32),
             pltpu.VMEM((PHASES, SLOTS, 8, LANES), f32),
-            pltpu.VMEM((PHASES, SLOTS, 8, LANES), f32),
+            pltpu.VMEM((2, PHASES * GROUP_ROWS, LANES), f32),
+            pltpu.SemaphoreType.DMA((GROUPS // PHASES,)),
+            pltpu.SemaphoreType.DMA((2,)),
         ],
-        compiler_params=pltpu.CompilerParams(vmem_limit_bytes=32 * 1024 * 1024),
-        cost_estimate=pl.CostEstimate(flops=7_000_000, bytes_accessed=8_000_000, transcendentals=10_000),
-    )(packed, sums, depth, wind, flags, trig, tables)
+        compiler_params=pltpu.CompilerParams(vmem_limit_bytes=56 * 1024 * 1024),
+        cost_estimate=pl.CostEstimate(flops=1_000_000, bytes_accessed=8_000_000, transcendentals=10_000),
+    )(packed, sums, depth, flags, tables)
 
 
 def tile_rows(array):
@@ -638,8 +662,10 @@
     trig = jnp.asarray(np.stack([np.cos(angle), np.sin(angle)]).astype(np.float32))
     tables = jnp.asarray(phase_tables())
     depth_rows = tile_rows(depth)
-    packed, sums = move(lines, tile_rows(spectrum), tile_rows(current), depth_rows, sea_blocks, trig, tables)
-    out = relax(packed, sums, depth_rows, tile_rows(wind), sea_blocks, trig, tables)
+    packed, sums = move(
+        lines, tile_rows(spectrum), tile_rows(current), depth_rows, tile_rows(wind), sea_blocks, trig, tables
+    )
+    out = relax(packed, sums, depth_rows, sea_blocks, tables)
     return jnp.swapaxes(out.reshape(-1, 4, 4, LANES), 1, 2).reshape(spectrum.shape)
 
 

time: 115 us -> 110 us (0.957)
  Pallas kernels: 111 us -> 108 us
  local copies, waits for them, and re-layouts: 2.47 us -> 0 us
    unnamed x14 -> x0, local copies, waits for them, and re-layouts: 2.47 us -> none
    pallas_call x1, Pallas kernels: 104 us -> 102 us  [move(): pl.pallas_call(functools.partial(move_kernel, lines), out_shape=(jax.Shap...]
where the time goes in v3:
time: 110 us; the launch traced here: 108 us
  Pallas kernels  108 us (98%)
    pallas_call x1, Pallas kernels, move(): pl.pallas_call(functools.partial(move_kernel, lines), out_shape=(jax.Shap...  102 us
    pallas_call x1, Pallas kernels, relax(): pl.pallas_call(relax_kernel, out_shape=jax.ShapeDtypeStruct((GROUPS * GRO...  6.53 us

profile of v3, /device:TPU:4, one launch (start us, length us, event | category | flops | bytes accessed | tf_op | source)
XLA Modules:
  0.0 108.5 jit_solution(273262826210675114)
XLA Ops:
  0.0 101.9 %shard_map.73 = (f32[5184,128]{1,0:T(8,128)}, f32[24,128]{1,0:T(8,128)}) custom-call(f32[10368,128]{1,0:T(8,128)} %bitcast.25, f32[32,128]{1,0:T(8,128)} %bitcast.28, f32[16,128]{1,0:T(8,128)} %bitcast.26, f32[32,128]{1,0:T(8,128)} %bitcast.29, s32[4,4]{1,0:T(4,128)} %flags.3, f32[2,37]{1,0:T(2,128)} %constant.4.clone.trig, ...), custom_call_target="tpu_custom_call" | custom-call | flops 250000000 | bytes 16000000 | tf_op jit(solution)/shard_map/pallas_call | solution.py:512
  101.9 6.5 %shard_map.74 = f32[10368,128]{1,0:T(8,128)} custom-call(f32[5184,128]{1,0:T(8,128)} %get-tuple-element.7.packed, f32[24,128]{1,0:T(8,128)} %get-tuple-element.8.sums, f32[16,128]{1,0:T(8,128)} %bitcast.27, s32[4,4]{1,0:T(4,128)} %flags.3, f32[3,9,8,128]{3,2,1,0:T(8,128)} %constant.5.clone.tables), custom_call_target="tpu_custom_call" | custom-call | flops 1000000 | bytes 8000000 | tf_op jit(solution)/shard_map/pallas_call | solution.py:637

commit v4 on v3

--- a/solution.py
+++ b/solution.py
@@ -31,6 +31,7 @@
 CHUNKS = ((0, 2), (2, 3), (5, 3), (8, 3), (11, 3), (14, 2), (16, 2), (18, 1), (19, 1), (20, 1))
 LAST = len(CHUNKS) - 1
 EARLY = 4
+BUFFERS = 9
 PHASES = 9
 TILES = LINE + 2
 BLOCKS = 16
@@ -130,6 +131,7 @@
     ids_recv,
     sum_send,
     sum_recv,
+    keep_sem,
     local_sem,
 ):
     space = lax.axis_index("space")
@@ -447,6 +449,13 @@
         for s in slices(c):
             into(c, s, place).wait_send()
 
+    split = CHUNKS[LAST - 2][0]
+
+    def keep(late, s):
+        begin, end = (split, SLICE + (s == LINE - 1)) if late else (0, split)
+        part = pl.ds((SLICE * s + begin) * PACK_ROWS, (end - begin) * PACK_ROWS)
+        return pltpu.make_async_copy(returned.at[part], packed_out.at[part], keep_sem.at[late, s])
+
     totals = (jnp.zeros((8, LANES), jnp.float32),) * (3 * SLOTS)
     for c in (*range(EARLY), LAST, *range(EARLY, LAST)):
         for s in slices(c):
@@ -473,8 +482,11 @@
 
         first, count = CHUNKS[c]
         totals = lax.fori_loop(first, first + count, add, totals)
-    keep = pltpu.make_async_copy(returned, packed_out, local_sem)
-    keep.start()
+        if c == LAST - 3:
+            for s in range(LINE):
+                keep(0, s).start()
+    for s in range(LINE):
+        keep(1, s).start()
     for q in range(3 * SLOTS):
         sums_mine[pl.ds(q, 1), :] = jnp.sum(totals[q], axis=0, keepdims=True)
     swap = remote(sums_mine, sums_other, sum_send, sum_recv, (space, other))
@@ -493,7 +505,9 @@
         for i in range(LINE):
             back(LAST, i, place).wait_send()
 
-    keep.wait()
+    for s in range(LINE):
+        keep(0, s).wait()
+        keep(1, s).wait()
     swap.wait()
     sums_out[...] = sums_mine[...] + sums_other[...]
 
@@ -561,6 +575,7 @@
             dma((LINE,)),
             dma,
             dma,
+            dma((2, LINE)),
             dma,
         ],
         compiler_params=pltpu.CompilerParams(
@@ -570,7 +585,25 @@
     )(spectrum, current, depth, wind, flags, trig, tables)
 
 
-def relax_kernel(packed, sums, depths, flags, tables, out, loaded, ids, brake, staged, in_sems, out_sems):
+def relax_kernel(
+    packed,
+    sums_from,
+    depths_from,
+    flags_from,
+    tables_from,
+    out,
+    loaded,
+    sums,
+    depths,
+    flags,
+    sigma,
+    ids,
+    brake,
+    staged,
+    small_sems,
+    in_sems,
+    out_sems,
+):
     span_in, span_out = PHASES * PACK_ROWS, PHASES * GROUP_ROWS
     steps = GROUPS // PHASES
 
@@ -579,12 +612,23 @@
         return pltpu.make_async_copy(packed.at[part], loaded.at[part], in_sems.at[j])
 
     def copy_out(j):
-        here = lax.rem(j, 2)
+        here = lax.rem(j, BUFFERS)
         part = pl.ds(pl.multiple_of(j * span_out, 8), span_out)
         return pltpu.make_async_copy(staged.at[here], out.at[part], out_sems.at[here])
 
+    small = [
+        pltpu.make_async_copy(flags_from, flags, small_sems.at[0]),
+        pltpu.make_async_copy(depths_from, depths, small_sems.at[1]),
+        pltpu.make_async_copy(tables_from.at[0], sigma, small_sems.at[2]),
+        pltpu.make_async_copy(sums_from, sums, small_sems.at[3]),
+    ]
+    for copy in small:
+        copy.start()
     for j in range(steps):
         copy_in(j).start()
+    staged[...] = jnp.zeros(staged.shape, jnp.float32)
+    for copy in small:
+        copy.wait()
 
     total = jnp.int32(0)
     for blk in range(BLOCKS):
@@ -595,7 +639,6 @@
         ids[jnp.where(flag > 0, found, dry)] = blk
         found = found + flag
         dry = dry + 1 - flag
-    staged[...] = jnp.zeros(staged.shape, jnp.float32)
     for slot in range(SLOTS):
         here = sums[pl.ds(slot, 1), :]
         mean_sigma = (here + EPSILON) / (sums[pl.ds(SLOTS + slot, 1), :] + EPSILON)
@@ -606,16 +649,18 @@
         depth = jnp.broadcast_to(depths[pl.ds(ids[slot], 1), :], (8, LANES))
         at_sea = jnp.where(slot < total, 1.0, 0.0)
         for p in range(PHASES):
-            wavenum = wave_number(tables[0, p] * tables[0, p], depth)
+            wavenum = wave_number(sigma[p] * sigma[p], depth)
             brake[p, slot] = at_sea / (1.0 + rate * wavenum)
 
     def step(j, carry):
-        @pl.when(j >= 2)
-        def _():
-            copy_out(j - 2).wait()
+        if BUFFERS < steps:
+
+            @pl.when(j >= BUFFERS)
+            def _():
+                copy_out(j - BUFFERS).wait()
 
         copy_in(j).wait()
-        here = lax.rem(j, 2)
+        here = lax.rem(j, BUFFERS)
         for q in range(PHASES):
             for slot in range(SLOTS):
                 row = pl.multiple_of(j * span_in + (q * SLOTS + slot) * 8, 8)
@@ -625,27 +670,30 @@
         return carry
 
     lax.fori_loop(0, steps, step, 0)
-    copy_out(steps - 2).wait()
-    copy_out(steps - 1).wait()
+    for j in range(steps - BUFFERS, steps):
+        copy_out(j).wait()
 
 
 def relax(packed, sums, depth, flags, tables):
-    vmem = pl.BlockSpec(memory_space=pltpu.VMEM)
-    smem = pl.BlockSpec(memory_space=pltpu.SMEM)
     hbm = pl.BlockSpec(memory_space=pl.ANY)
     f32 = jnp.float32
     return pl.pallas_call(
         relax_kernel,
         out_shape=jax.ShapeDtypeStruct((GROUPS * GROUP_ROWS, LANES), f32),
-        in_specs=[hbm, vmem, vmem, smem, vmem],
+        in_specs=[hbm] * 5,
         out_specs=hbm,
         scratch_shapes=[
             pltpu.VMEM((GROUPS * PACK_ROWS, LANES), f32),
+            pltpu.VMEM((3 * SLOTS, LANES), f32),
+            pltpu.VMEM((BLOCKS, LANES), f32),
+            pltpu.SMEM((4, 4), jnp.int32),
+            pltpu.VMEM((PHASES, 8, LANES), f32),
             pltpu.SMEM((BLOCKS,), jnp.int32),
             pltpu.VMEM((PHASES, SLOTS, 8, LANES), f32),
-            pltpu.VMEM((2, PHASES * GROUP_ROWS, LANES), f32),
+            pltpu.VMEM((BUFFERS, PHASES * GROUP_ROWS, LANES), f32),
+            pltpu.SemaphoreType.DMA((4,)),
             pltpu.SemaphoreType.DMA((GROUPS // PHASES,)),
-            pltpu.SemaphoreType.DMA((2,)),
+            pltpu.SemaphoreType.DMA((BUFFERS,)),
         ],
         compiler_params=pltpu.CompilerParams(vmem_limit_bytes=56 * 1024 * 1024),
         cost_estimate=pl.CostEstimate(flops=1_000_000, bytes_accessed=8_000_000, transcendentals=10_000),

time: 110 us -> 107 us (0.973)
  Pallas kernels: 108 us -> 106 us
    pallas_call x1, Pallas kernels: 6.53 us -> 4.38 us  [relax(): pl.pallas_call(relax_kernel, out_shape=jax.ShapeDtypeStruct((GROUPS * GRO...]
where the time goes in v4:
time: 107 us; the launch traced here: 106 us
  Pallas kernels  106 us (99%)
    pallas_call x1, Pallas kernels, move(): pl.pallas_call(functools.partial(move_kernel, lines), out_shape=(jax.Shap...  102 us
    pallas_call x1, Pallas kernels, relax(): pl.pallas_call(relax_kernel, out_shape=jax.ShapeDtypeStruct((GROUPS * GRO...  4.38 us

profile of v4, /device:TPU:4, one launch (start us, length us, event | category | flops | bytes accessed | tf_op | source)
XLA Modules:
  0.0 106.4 jit_solution(1218118394523834311)
XLA Ops:
  0.0 102.0 %shard_map.73 = (f32[5184,128]{1,0:T(8,128)}, f32[24,128]{1,0:T(8,128)}) custom-call(f32[10368,128]{1,0:T(8,128)} %bitcast.25, f32[32,128]{1,0:T(8,128)} %bitcast.28, f32[16,128]{1,0:T(8,128)} %bitcast.26, f32[32,128]{1,0:T(8,128)} %bitcast.29, s32[4,4]{1,0:T(4,128)} %flags_from.1, f32[2,37]{1,0:T(2,128)} %constant.4.clone.trig, ...), custom_call_target="tpu_custom_call" | custom-call | flops 250000000 | bytes 16000000 | tf_op jit(solution)/shard_map/pallas_call | solution.py:526
  102.0 4.4 %shard_map.74 = f32[10368,128]{1,0:T(8,128)} custom-call(f32[5184,128]{1,0:T(8,128)} %get-tuple-element.7.packed, f32[24,128]{1,0:T(8,128)} %get-tuple-element.8.sums_from, f32[16,128]{1,0:T(8,128)} %bitcast.27, s32[4,4]{1,0:T(4,128)} %flags_from.1, f32[3,9,8,128]{3,2,1,0:T(8,128)} %constant.5.clone.tables.tables_from), custom_call_target="tpu_custom_call" | custom-call | flops 1000000 | bytes 8000000 | tf_op jit(solution)/shard_map/pallas_call | solution.py:680

commit v5 on v4

--- a/solution.py
+++ b/solution.py
@@ -80,14 +80,18 @@
 def move_kernel(
     lines,
     spectrum,
-    current,
-    depth_here,
+    current_from,
+    depth_from,
+    winds_from,
+    flags_from,
+    trig_from,
+    tables_from,
+    packed_out,
+    sums_out,
     winds,
     flags,
     trig,
     tables,
-    packed_out,
-    sums_out,
     fields,
     ids,
     ids_here,
@@ -132,6 +136,7 @@
     sum_send,
     sum_recv,
     keep_sem,
+    small_sem,
     local_sem,
 ):
     space = lax.axis_index("space")
@@ -148,9 +153,20 @@
     for peer in members + [above, below]:
         pl.semaphore_signal(barrier, inc=1, device_id=peer, device_id_type=MESH)
 
+    small = [
+        pltpu.make_async_copy(flags_from, flags, small_sem.at[0]),
+        pltpu.make_async_copy(current_from, fields.at[pl.ds(0, 2 * BLOCKS)], small_sem.at[1]),
+        pltpu.make_async_copy(depth_from, fields.at[pl.ds(2 * BLOCKS, BLOCKS)], small_sem.at[2]),
+        pltpu.make_async_copy(tables_from, tables, small_sem.at[3]),
+        pltpu.make_async_copy(winds_from, winds, small_sem.at[4]),
+        pltpu.make_async_copy(trig_from, trig, small_sem.at[5]),
+    ]
+    for copy in small:
+        copy.start()
+    for copy in small:
+        copy.wait()
+
     lane = lax.broadcasted_iota(jnp.int32, (8, LANES), 1)
-    fields[: 2 * BLOCKS] = current[...]
-    fields[2 * BLOCKS : 3 * BLOCKS] = depth_here[...]
     numbers = jnp.zeros((8, LANES), jnp.int32)
     found = jnp.int32(0)
     for blk in range(BLOCKS):
@@ -514,7 +530,6 @@
 
 def move(lines, spectrum, current, depth, wind, flags, trig, tables):
     vmem = pl.BlockSpec(memory_space=pltpu.VMEM)
-    smem = pl.BlockSpec(memory_space=pltpu.SMEM)
     hbm = pl.BlockSpec(memory_space=pl.ANY)
     f32 = jnp.float32
     dma = pltpu.SemaphoreType.DMA
@@ -529,9 +544,13 @@
             jax.ShapeDtypeStruct((GROUPS * PACK_ROWS, LANES), f32),
             jax.ShapeDtypeStruct((3 * SLOTS, LANES), f32),
         ),
-        in_specs=[hbm, vmem, vmem, vmem, smem, smem, vmem],
+        in_specs=[hbm] * 7,
         out_specs=(hbm, vmem),
         scratch_shapes=[
+            pltpu.VMEM((2 * BLOCKS, LANES), f32),
+            pltpu.SMEM((4, 4), jnp.int32),
+            pltpu.SMEM((2, ND + 1), f32),
+            tiles(3, PHASES),
             pltpu.VMEM((4 * BLOCKS, LANES), f32),
             pltpu.VMEM((8, LANES), jnp.int32),
             pltpu.SMEM((8, LANES), jnp.int32),
@@ -576,6 +595,7 @@
             dma,
             dma,
             dma((2, LINE)),
+            dma((6,)),
             dma,
         ],
         compiler_params=pltpu.CompilerParams(

time: 107 us -> 106 us (level)
  no operation moved by 1% of the time
where the time goes in v5:
time: 106 us; the launch traced here: 105 us
  Pallas kernels  105 us (99%)
    pallas_call x1, Pallas kernels, move(): pl.pallas_call(functools.partial(move_kernel, lines), out_shape=(jax.Shap...  101 us
    pallas_call x1, Pallas kernels, relax(): pl.pallas_call(relax_kernel, out_shape=jax.ShapeDtypeStruct((GROUPS * GRO...  4.38 us

profile of v5, /device:TPU:4, one launch (start us, length us, event | category | flops | bytes accessed | tf_op | source)
XLA Modules:
  0.0 105.5 jit_solution(10479630104444209239)
XLA Ops:
  0.0 101.1 %shard_map.73 = (f32[5184,128]{1,0:T(8,128)}, f32[24,128]{1,0:T(8,128)}) custom-call(f32[10368,128]{1,0:T(8,128)} %bitcast.25, f32[32,128]{1,0:T(8,128)} %bitcast.28, f32[16,128]{1,0:T(8,128)} %bitcast.26, f32[32,128]{1,0:T(8,128)} %bitcast.29, s32[4,4]{1,0:T(4,128)} %flags_from.3, f32[2,37]{1,0:T(2,128)} %constant.4.clone.trig_from, ...), custom_call_target="tpu_custom_call" | custom-call | flops 250000000 | bytes 16000000 | tf_op jit(solution)/shard_map/pallas_call | solution.py:541
  101.1 4.4 %shard_map.74 = f32[10368,128]{1,0:T(8,128)} custom-call(f32[5184,128]{1,0:T(8,128)} %get-tuple-element.7.packed, f32[24,128]{1,0:T(8,128)} %get-tuple-element.8.sums_from, f32[16,128]{1,0:T(8,128)} %bitcast.27, s32[4,4]{1,0:T(4,128)} %flags_from.3, f32[3,9,8,128]{3,2,1,0:T(8,128)} %constant.5.clone.tables_from), custom_call_target="tpu_custom_call" | custom-call | flops 1000000 | bytes 8000000 | tf_op jit(solution)/shard_map/pallas_call | solution.py:700

commit v6 on v5

--- a/solution.py
+++ b/solution.py
@@ -473,7 +473,7 @@
         return pltpu.make_async_copy(returned.at[part], packed_out.at[part], keep_sem.at[late, s])
 
     totals = (jnp.zeros((8, LANES), jnp.float32),) * (3 * SLOTS)
-    for c in (*range(EARLY), LAST, *range(EARLY, LAST)):
+    for c in range(LAST + 1):
         for s in slices(c):
             back(c, s, s).wait_recv()
 

time: 106 us -> 106 us (level)
  no operation moved by 1% of the time
where the time goes in v6:
time: 106 us; the launch traced here: 105 us
  Pallas kernels  105 us (99%)
    pallas_call x1, Pallas kernels, move(): pl.pallas_call(functools.partial(move_kernel, lines), out_shape=(jax.Shap...  101 us
    pallas_call x1, Pallas kernels, relax(): pl.pallas_call(relax_kernel, out_shape=jax.ShapeDtypeStruct((GROUPS * GRO...  4.38 us

profile of v6, /device:TPU:4, one launch (start us, length us, event | category | flops | bytes accessed | tf_op | source)
XLA Modules:
  0.0 105.4 jit_solution(4205487629310320895)
XLA Ops:
  0.0 101.0 %shard_map.73 = (f32[5184,128]{1,0:T(8,128)}, f32[24,128]{1,0:T(8,128)}) custom-call(f32[10368,128]{1,0:T(8,128)} %bitcast.25, f32[32,128]{1,0:T(8,128)} %bitcast.28, f32[16,128]{1,0:T(8,128)} %bitcast.26, f32[32,128]{1,0:T(8,128)} %bitcast.29, s32[4,4]{1,0:T(4,128)} %flags_from.3, f32[2,37]{1,0:T(2,128)} %constant.4.clone.trig_from, ...), custom_call_target="tpu_custom_call" | custom-call | flops 250000000 | bytes 16000000 | tf_op jit(solution)/shard_map/pallas_call | solution.py:541
  101.0 4.4 %shard_map.74 = f32[10368,128]{1,0:T(8,128)} custom-call(f32[5184,128]{1,0:T(8,128)} %get-tuple-element.7.packed, f32[24,128]{1,0:T(8,128)} %get-tuple-element.8.sums_from, f32[16,128]{1,0:T(8,128)} %bitcast.27, s32[4,4]{1,0:T(4,128)} %flags_from.3, f32[3,9,8,128]{3,2,1,0:T(8,128)} %constant.5.clone.tables_from), custom_call_target="tpu_custom_call" | custom-call | flops 1000000 | bytes 8000000 | tf_op jit(solution)/shard_map/pallas_call | solution.py:700
